TPU v7x, 256 devices: a whole 4x4x8 slice. The times are simulated.
256 devices in a mesh: tensor: 8 (over x, y_lo), seq: 32 (over y_hi, z, core).
Axes of the slice: x: 4, y: 4 (y_hi: 2, y_lo: 2; y = y_hi * 2 + y_lo), z: 8, core: 2. Of those that a mesh axis runs over, the one named last changes fastest.
Arguments:
- tokens: bfloat16 [32, 1024, 5120], P('seq', 'tensor'), may hold values from -6 to 6
- query_weight: bfloat16 [5120, 1024], P(None, 'tensor'), may hold values from -0.078125 to 0.078125
- key_weight: bfloat16 [5120, 1024], P(None, 'tensor'), may hold values from -0.078125 to 0.078125
- value_weight: bfloat16 [5120, 5120], P(None, 'tensor'), may hold values from -0.078125 to 0.078125
- conv_taps: float32 [3, 5120], P(None, 'tensor'), may hold values from 0.2 to 2
- norm_gain: float32 [5120], P('tensor'), may hold values from 8 to 64
Outputs:
- mixed: bfloat16 [32, 1024, 5120], P('seq', 'tensor')
All inputs are finite; a program needn't handle non-finite values.
Results may differ from a plain program's by a relative error of at most 0.012.
Values may be sent and summed in bfloat16 or wider, within the bound.
No kernel may reach another device: no remote copies, remote signals or barrier semaphores. Data moves between devices by JAX's collectives and lax.ppermute only.
A program may use at most 128 MiB of HBM per device.

v0:
```python
import jax
import jax.numpy as jnp
from jax import lax
from jax.sharding import PartitionSpec as P

FEAT = 16


def padded_2(block, sides, width):
    for axis, dim in sides:
        count = lax.axis_size(axis)
        forward = [(i, i + 1) for i in range(count - 1)]
        backward = [(target, source) for source, target in forward]
        low = lax.ppermute(
            lax.slice_in_dim(block, block.shape[dim] - width, None, axis=dim), axis, forward
        )
        high = lax.ppermute(lax.slice_in_dim(block, 0, width, axis=dim), axis, backward)
        block = jnp.concatenate([low, block, high], axis=dim)
    return block


def expand_heads(scaled):
    head_count, feat_count, row_count = scaled.shape
    outer = (scaled[:, :, None, :] * scaled[:, None, :, :]).reshape(
        head_count, feat_count * feat_count, row_count
    )
    ones_row = jnp.ones((head_count, 1, row_count), jnp.float32)
    return jnp.concatenate([ones_row, scaled, outer * 0.5**0.5], axis=1)


def body(tokens, query_weight, key_weight, value_weight, conv_taps, norm_gain):
    inputs = tokens.reshape(-1, tokens.shape[-1])
    query_cols = query_weight.shape[1]
    gathered = lax.all_gather(inputs, "tensor", axis=0, tiled=True)
    queries = jnp.dot(gathered, query_weight, preferred_element_type=jnp.float32)
    keys_full = jnp.dot(gathered, key_weight, preferred_element_type=jnp.float32)
    values = jnp.dot(gathered, value_weight, preferred_element_type=jnp.float32).astype(
        jnp.bfloat16
    )
    row_count = queries.shape[0]
    head_count = query_cols // FEAT
    value_cols = value_weight.shape[1]
    head_width = value_cols // head_count
    reach = conv_taps.shape[0] // 2
    padded = padded_2(values, (("seq", 0),), reach)
    conv_sum = jnp.zeros((row_count, value_cols), jnp.float32)
    for offset in range(conv_taps.shape[0]):
        conv_sum = conv_sum + conv_taps[offset] * padded[offset : offset + row_count].astype(
            jnp.float32
        )
    conv = conv_sum.astype(jnp.bfloat16)
    query_heads = (queries * 0.5).reshape(row_count, head_count, FEAT).transpose(1, 2, 0)
    key_heads = (keys_full * 0.5).reshape(row_count, head_count, FEAT).transpose(1, 2, 0)
    feat_query = expand_heads(query_heads).astype(jnp.bfloat16)
    feat_key = expand_heads(key_heads).astype(jnp.bfloat16)
    value_heads = conv.reshape(row_count, head_count, head_width)
    state = jnp.einsum("hfr,rhd->hfd", feat_key, value_heads, preferred_element_type=jnp.float32)
    total = jnp.sum(feat_key.astype(jnp.float32), axis=2)
    flat_state, flat_total = lax.psum((state.reshape(-1), total.reshape(-1)), "seq")
    state_low = flat_state.reshape(state.shape).astype(jnp.bfloat16)
    total = flat_total.reshape(total.shape)
    numer = jnp.einsum("hfr,hfd->rhd", feat_query, state_low, preferred_element_type=jnp.float32)
    denom = jnp.einsum(
        "hfr,hf->rh", feat_query.astype(jnp.float32), total, precision=lax.Precision.HIGHEST
    )
    attn = (numer / denom[:, :, None]).reshape(row_count, value_cols)
    mixed = (attn * norm_gain + conv.astype(jnp.float32)).astype(jnp.bfloat16)
    result = lax.all_to_all(mixed, "tensor", split_axis=0, concat_axis=1, tiled=True)
    return result.reshape(tokens.shape[0], tokens.shape[1], result.shape[1])


def solution(mesh):
    return jax.shard_map(
        body,
        mesh=mesh,
        in_specs=(
            P("seq", "tensor", None),
            P(None, "tensor"),
            P(None, "tensor"),
            P(None, "tensor"),
            P(None, "tensor"),
            P("tensor"),
        ),
        out_specs=P("seq", "tensor", None),
        check_vma=False,
    )
```

profile of v0, /device:TPU:1, one launch (start us, length us, event | category | flops | bytes accessed | tf_op | source)
XLA Modules:
  0.0 447.0 jit_solution(15982859838991781854)
XLA Ops:
  6.5 0.7 all-gather.3.cloned.1.call-update
  7.3 0.8 slice_reduce_fusion.2
  8.1 215.1 %all-gather.3.cloned.1.call-done = bf16[1,1024,5120]{2,1,0:T(8,128)(2,1)} async-done(((bf16[1,128,5120]{2,1,0:T(8,128)(2,1)}), bf16[1,1024,5120]{2,1,0:T(8,128)(2,1)}) %all-gather.3.cloned.1.call-update) | async-done | bytes 10485776 | tf_op jit(solution)/shard_map/all_gather | solution.py:34
  223.2 13.0 %fusion.12 = bf16[1024,640]{1,0:T(8,128)(2,1)S(1)} fusion(bf16[5120,640]{1,0:T(8,128)(2,1)} %param.9, bf16[1,1024,5120]{2,1,0:T(8,128)(2,1)} %all-gather.3.cloned.1.call-done), kind=kOutput, calls=%fused_computation.20 | convolution fusion | flops 6711541760 | bytes 18350080 | tf_op jit(solution)/shard_map/dot_general | solution.py:37
  236.2 3.7 collective-permute-start
  240.0 2.1 collective-permute-start.1
  242.1 3.6 bitcast_convert_fusion
  245.7 1.4 multiply_convert_fusion.1
  247.1 0.0 copy-start.2
  247.1 0.0 copy-start.4
  247.1 1.9 copy-done.2
  249.1 2.1 convert_reduce_fusion
  251.2 3.6 fusion.18
  254.8 3.3 multiply_convert_fusion
  258.0 0.7 convert.20
  258.8 0.0 collective-permute-done
  258.8 0.0 collective-permute-done.1
  258.8 2.0 add_convert_fusion.1
  260.8 2.5 copy.10
  263.3 5.2 %fusion.6 = f32[8,273,80]{2,1,0:T(8,128)} fusion(bf16[1024,8,80]{0,2,1:T(8,128)(2,1)} %bitcast.52, bf16[8,256,1024]{2,1,0:T(8,128)(2,1)} %bitcast.43, bf16[8,16,1024]{2,1,0:T(8,128)(2,1)S(1)} %get-tuple-element.12, bf16[273]{0:T(512)(128)(2,1)S(1)} %pad.7.clone), kind=kOutput, calls=%fused_computation.14 | convolution fusion | flops 371245056 | bytes 6466594 | tf_op jit(solution)/shard_map/hfr,rhd->hfd/dot_general | solution.py:57
  268.5 2.0 reshape.56
  270.5 134.8 %all-reduce.2 = (f32[8,273]{1,0:T(8,128)S(1)}, bf16[174720]{0:T(1024)(128)(2,1)}) all-reduce(f32[8,273]{1,0:T(8,128)S(1)} %convert_reduce_fusion, f32[174720]{0:T(1024)S(1)} %reshape.56), channel_id=1, replica_groups=mesh['tensor'=8,'seq'=32] {'seq'}, use_global_device_ids=true, to_apply=%region_2.0 | all-reduce | flops 176904 | bytes 1065792 | tf_op jit(solution)/shard_map/psum | solution.py:59
  405.3 1.8 convert_element_type.39
  407.1 0.0 copy-start.3
  407.1 0.0 copy-start.5
  407.1 5.3 %fusion.7 = f32[8,1,1024]{2,1,0:T(1,128)S(1)} fusion(bf16[8,256,1024]{2,1,0:T(8,128)(2,1)} %bitcast.49, bf16[8,16,1024]{2,1,0:T(8,128)(2,1)} %convert.20, bf16[273]{0:T(512)(128)(2,1)S(1)} %pad.7.clone, f32[8,273,1]{1,0,2:T(8,128)S(1)} %bitcast.54), kind=kOutput, calls=%fused_computation.15 | convolution fusion | flops 40255488 | bytes 4498498 | tf_op jit(solution)/shard_map/hfr,hf->rh/dot_general | solution.py:63
  412.4 3.3 bitcast_divide_fusion
  415.7 3.3 copy.13
  418.9 2.8 add_convert_fusion
  421.8 16.2 %all_to_all.16 = bf16[8,128,640]{2,1,0:T(8,128)(2,1)S(1)} all-to-all(bf16[8,128,640]{2,1,0:T(8,128)(2,1)S(1)} %bitcast.48), channel_id=1, replica_groups=mesh['tensor'=8,'seq'=32] {'tensor'}, dimensions={0} | all-to-all | bytes 2621440 | tf_op jit(solution)/shard_map/all_to_all | solution.py:68
  437.9 0.7 copy.14
  438.7 1.5 reshape.61
  (13 shorter events, 0.0 us)
Async XLA Ops:
  6.5 235.6 %copy-start = (bf16[5120,128]{1,0:T(8,128)(2,1)S(1)}, bf16[5120,128]{1,0:T(8,128)(2,1)}, u32[]{:S(2)}) copy-start(bf16[5120,128]{1,0:T(8,128)(2,1)} %param.8) | copy-start | bytes 3932164
  6.5 216.7 %all-gather.3.cloned.1.call-start = ((), (), s32[]{:S(2)}) async-start(), calls=%async_computation.1 | async-start | bytes 11796480 | tf_op jit(solution)/shard_map/all_gather | solution.py:34
  223.2 18.9 %copy-start.1 = (bf16[1,1024,5120]{2,1,0:T(8,128)(2,1)S(1)}, bf16[1,1024,5120]{2,1,0:T(8,128)(2,1)}, u32[]{:S(2)}) copy-start(bf16[1,1024,5120]{2,1,0:T(8,128)(2,1)} %all-gather.3.cloned.1.call-done) | copy-start | bytes 31457284
  236.2 22.5 %collective-permute-start = (bf16[1,640]{1,0:T(2,128)(2,1)S(1)}, bf16[1,640]{1,0:T(2,128)(2,1)S(1)}, u32[]{:S(2)}, u32[]{:S(2)}) collective-permute-start(bf16[1,640]{1,0:T(2,128)(2,1)S(1)} %get-tuple-element.10), channel_id=1, source_target_pairs={{0,1},{1,2},{2,3},{3,4},{4,5},{5,6},{6,7},{7,8},{8,9},{9,10},{10,1... | collective-permute-start | bytes 3848 | tf_op jit(solution)/shard_map/ppermute | solution.py:14
  240.0 18.8 %collective-permute-start.1 = (bf16[1,640]{1,0:T(2,128)(2,1)S(1)}, bf16[1,640]{1,0:T(2,128)(2,1)S(1)}, u32[]{:S(2)}, u32[]{:S(2)}) collective-permute-start(bf16[1,640]{1,0:T(2,128)(2,1)S(1)} %get-tuple-element.11), channel_id=1, source_target_pairs={{1,0},{2,1},{3,2},{4,3},{5,4},{6,5},{7,6},{8,7},{9,8},{10,9},{11,1... | collective-permute-start | bytes 3848 | tf_op jit(solution)/shard_map/ppermute | solution.py:17
  247.1 2.0 copy-start.2
  247.1 4.1 copy-start.4
  407.1 5.3 %copy-start.3 = (bf16[8,16,16,1024]{3,2,1,0:T(8,128)(2,1)S(1)}, bf16[8,16,16,1024]{3,2,1,0:T(8,128)(2,1)}, u32[]{:S(2)}) copy-start(bf16[8,16,16,1024]{3,2,1,0:T(8,128)(2,1)} %multiply_convert_fusion) | copy-start | bytes 12582916
  407.1 5.3 %copy-start.5 = (bf16[8,16,1024]{2,1,0:T(8,128)(2,1)S(1)}, bf16[8,16,1024]{2,1,0:T(8,128)(2,1)}, u32[]{:S(2)}) copy-start(bf16[8,16,1024]{2,1,0:T(8,128)(2,1)} %convert.20) | copy-start | bytes 786436
  415.7 3.3 copy-start.6
Sparse Core Ops, SparseCore 0:
  9.1 214.0 all-gather.2
where the time goes:
time: 453 us; the launch traced here: 447 us
  waiting for transfers between devices  216 us (48%)
  blocking collectives  151 us (33%)
  matrix products  33.9 us (7%)
  local copies, waits for them, and re-layouts  14.6 us (3%)
  between operations  13.6 us (3%)
  other arithmetic  12.3 us (3%)
  starting transfers between devices  5.85 us (1%)
    all_gather x1, waiting for transfers between devices, body(): gathered = lax.all_gather(inputs, 'tensor', axis=0, tiled=True)  215 us
    psum x1, blocking collectives, body(): lax.psum((state.reshape(-1), total.reshape(-1)), 'seq')  135 us
    all_to_all x1, blocking collectives, body(): lax.all_to_all(mixed, 'tensor', split_axis=0, concat_axis=1, tiled=True)  16.2 us
    dot_general x1, matrix products, body(): jnp.dot(gathered, value_weight, preferred_element_type=jnp.float32)  13 us
  transfers between devices with their start and end apart: 3, of which 1 were waited for; matrix products, arithmetic and copies ran while one was open for 3% of the time, Pallas kernels for 0%

commit v1 on v0

v1 whole, which is shorter than its diff:
```python
import functools

import jax
import jax.numpy as jnp
from jax import lax
from jax.experimental import pallas as pl
from jax.experimental.pallas import tpu as pltpu
from jax.sharding import PartitionSpec as P

FEAT = 16
HEAD_DIM = 80
GROUP = 8
NX, NY, NZ = 4, 4, 8
AXES = ("tensor", "seq")
PIECE = 512
FROWS = 160
MROWS = 192
BLOCK = 128
ROWS = 4 * BLOCK
HALO = 16
VCOLS = GROUP * HEAD_DIM
QCOLS = GROUP * FEAT
GCOLS = VCOLS + 2 * QCOLS
SPLIT = MROWS // NY


def device_of(x, y, z, core):
    x, y, z = x % NX, y % NY, z % NZ
    tensor = x * 2 + (y & 1)
    seq = ((y >> 1) * NZ + z) * 2 + core
    return tensor * 32 + seq


def everywhere():
    return [
        (x, y, z, core)
        for x in range(NX)
        for y in range(NY)
        for z in range(NZ)
        for core in range(2)
    ]


def receive(array, source_of):
    pairs = [(device_of(*source_of(*place)), device_of(*place)) for place in everywhere()]
    return lax.ppermute(array, AXES, pairs)


def from_x(array, step):
    return receive(array, lambda x, y, z, c: (x + step, y, z, c))


def from_y(array, step):
    return receive(array, lambda x, y, z, c: (x, y + step, z, c))


def from_z(array, step):
    return receive(array, lambda x, y, z, c: (x, y, z + step, c))


def from_core(array):
    return receive(array, lambda x, y, z, c: (x, y, z, 1 - c))


def from_block(array, step):
    place = {}
    for spot in everywhere():
        x, y, z, core = spot
        index = (((y >> 1) * NZ + z) * 2 + core) * 8 + x * 2 + (y & 1)
        place[index] = device_of(*spot)
    pairs = [(place[b + step], place[b]) for b in place if b + step in place]
    return lax.ppermute(array, AXES, pairs)


def features(scaled, off_weight):
    root = 0.5**0.5
    rows = scaled.shape[1]
    parts = [scaled, scaled * scaled * root]
    for step in range(1, FEAT // 2):
        turned = pltpu.roll(scaled, FEAT - step, 0)
        parts.append(scaled * turned * (root * off_weight))
    half = scaled[: FEAT // 2] * scaled[FEAT // 2 :] * (root * off_weight)
    parts.append(half)
    first = lax.broadcasted_iota(jnp.int32, (FEAT // 2, rows), 0) == 0
    parts.append(jnp.where(first, 1.0, 0.0).astype(jnp.float32))
    return jnp.concatenate(parts, axis=0)


def window_of(head):
    start = head * HEAD_DIM // 128 * 128
    stop = -(-(head + 1) * HEAD_DIM // 128) * 128
    return start, stop


def head_mask(head, rows):
    start, stop = window_of(head)
    lane = lax.broadcasted_iota(jnp.int32, (rows, stop - start), 1) + start
    return (lane >= head * HEAD_DIM) & (lane < (head + 1) * HEAD_DIM)


def project_body(x_copies, w_copies, taps, conv_out, query_out, state_out, xs, ws, acc, conv_scr):
    for copy in x_copies:
        copy.start()
    for group in w_copies:
        for copy in group:
            copy.start()
    for copy in x_copies:
        copy.wait()
    for copies in w_copies:
        for copy in copies:
            copy.wait()
    depth = xs.shape[1]
    acc[...] = jnp.zeros_like(acc)

    def step(index, carry):
        span = pl.ds(pl.multiple_of(index * PIECE, PIECE), PIECE)
        acc[...] += jnp.dot(xs[:, span], ws[span, :], preferred_element_type=jnp.float32)
        return carry

    lax.fori_loop(0, depth // PIECE, step, 0)

    query_out[...] = acc[:ROWS, :QCOLS].T * 0.5
    key = acc[:ROWS, QCOLS : 2 * QCOLS].T * 0.5
    values = acc[:, 2 * QCOLS :].astype(jnp.bfloat16).astype(jnp.float32)
    row = lax.broadcasted_iota(jnp.int32, (BLOCK, VCOLS), 0)
    for block in range(4):
        mid = values[block * BLOCK : (block + 1) * BLOCK]
        before = values[ROWS + 2 * block : ROWS + 2 * block + 1]
        after = values[ROWS + 2 * block + 1 : ROWS + 2 * block + 2]
        low = jnp.where(row == 0, before, pltpu.roll(mid, 1, 0))
        high = jnp.where(row == BLOCK - 1, after, pltpu.roll(mid, BLOCK - 1, 0))
        conv = taps[0:1, :] * low + taps[1:2, :] * mid + taps[2:3, :] * high
        conv_scr[block * BLOCK : (block + 1) * BLOCK, :] = conv.astype(jnp.bfloat16)
    conv_out[...] = conv_scr[...]
    state_out[...] = jnp.zeros_like(state_out)
    ones = jnp.ones((8, ROWS), jnp.bfloat16)
    for head in range(GROUP):
        feat = features(key[head * FEAT : (head + 1) * FEAT], 1.0).astype(jnp.bfloat16)
        start, stop = window_of(head)
        state = jnp.dot(feat, conv_scr[:, start:stop], preferred_element_type=jnp.float32)
        state_out[:FROWS, start:stop] += jnp.where(head_mask(head, FROWS), state, 0.0)
        total = lax.dot_general(
            ones, feat, (((1,), (1,)), ((), ())), preferred_element_type=jnp.float32
        )
        state_out[FROWS + head : FROWS + head + 1, :FROWS] = total[0:1]


def x_copies_of(x_refs, xs, sems):
    copies, at = [], 0
    for ref in x_refs:
        rows = ref.shape[0]
        copies.append(pltpu.make_async_copy(ref, xs.at[pl.ds(at, rows)], sems.at[len(copies)]))
        at += rows
    return copies


def own_kernel(x0, x1, x2a, x2b, x3, halo, qw, kw, vw, taps, conv_out, query_out, state_out, xs, ws, acc, conv_scr, xsem, wsem):
    copies = x_copies_of((x0, x1, x2a, x2b, x3, halo), xs, xsem)
    w_copies = [[
        pltpu.make_async_copy(qw, ws.at[:, pl.ds(0, QCOLS)], wsem.at[0]),
        pltpu.make_async_copy(kw, ws.at[:, pl.ds(QCOLS, QCOLS)], wsem.at[1]),
        pltpu.make_async_copy(vw, ws.at[:, pl.ds(2 * QCOLS, VCOLS)], wsem.at[2]),
    ]]
    project_body(copies, w_copies, taps, conv_out, query_out, state_out, xs, ws, acc, conv_scr)


def other_kernel(offsets, x0, x1, x2a, x2b, x3, halo, *rest):
    pieces, (taps, conv_out, query_out, state_out, xs, ws, acc, conv_scr, xsem, wsem) = rest[:-10], rest[-10:]
    copies = x_copies_of((x0, x1, x2a, x2b, x3, halo), xs, xsem)
    w_copies = []
    for index, piece in enumerate(pieces):
        span = pl.ds(pl.multiple_of(offsets[index], PIECE), PIECE)
        w_copies.append([pltpu.make_async_copy(piece, ws.at[span], wsem.at[index])])
    project_body(copies, w_copies, taps, conv_out, query_out, state_out, xs, ws, acc, conv_scr)


def project(kernel, scalars, blocks, weights, taps):
    depth = blocks[0].shape[1]
    rows = ROWS + HALO
    hbm = pl.BlockSpec(memory_space=pl.ANY)
    vmem = pl.BlockSpec(memory_space=pltpu.VMEM)
    return pl.pallas_call(
        kernel,
        out_shape=(
            jax.ShapeDtypeStruct((ROWS, VCOLS), jnp.bfloat16),
            jax.ShapeDtypeStruct((QCOLS, ROWS), jnp.float32),
            jax.ShapeDtypeStruct((MROWS, VCOLS), jnp.float32),
        ),
        in_specs=[pl.BlockSpec(memory_space=pltpu.SMEM)] * len(scalars)
        + [hbm] * (len(blocks) + len(weights))
        + [vmem],
        out_specs=(vmem, vmem, vmem),
        scratch_shapes=[
            pltpu.VMEM((rows, depth), jnp.bfloat16),
            pltpu.VMEM((depth, GCOLS), jnp.bfloat16),
            pltpu.VMEM((rows, GCOLS), jnp.float32),
            pltpu.VMEM((ROWS, VCOLS), jnp.bfloat16),
            pltpu.SemaphoreType.DMA((len(blocks),)),
            pltpu.SemaphoreType.DMA((max(len(weights), 1),)),
        ],
        compiler_params=pltpu.CompilerParams(vmem_limit_bytes=40 * 1024 * 1024),
        cost_estimate=pl.CostEstimate(
            flops=2 * rows * depth * GCOLS, bytes_accessed=2 * depth * (rows + GCOLS), transcendentals=0
        ),
    )(*scalars, *blocks, *weights, taps)


def attend_kernel(place, query_a, query_b, state_a, state_b, conv_a, conv_b, gain_a, gain_b, *rest):
    outs, acc = rest[:4], rest[4]
    groups = ((query_a, state_a, conv_a, gain_a), (query_b, state_b, conv_b, gain_b))
    for number, (query, state, conv, gain) in enumerate(groups):
        acc[...] = jnp.zeros_like(acc)
        totals = state[FROWS : FROWS + 16, :FROWS]
        for head in range(GROUP):
            feat = features(query[head * FEAT : (head + 1) * FEAT, :], 2.0)
            denom = jnp.dot(totals, feat.astype(jnp.bfloat16), preferred_element_type=jnp.float32)
            scale = 1.0 / denom[head : head + 1, :]
            scaled = (feat * scale).astype(jnp.bfloat16)
            start, stop = window_of(head)
            part = state[:FROWS, start:stop]
            part = jnp.where(head_mask(head, FROWS), part, jnp.zeros_like(part))
            acc[:, start:stop] += lax.dot_general(
                scaled, part, (((0,), (0,)), ((), ())), preferred_element_type=jnp.float32
            )
        spot = place[0] if number == 0 else 1 - place[0]
        span = pl.ds(pl.multiple_of(spot * VCOLS, VCOLS), VCOLS)
        for block, out in enumerate(outs):
            rows = slice(block * BLOCK, (block + 1) * BLOCK)
            mixed = acc[rows, :] * gain[0:1, :] + conv[rows, :].astype(jnp.float32)
            out[:, span] = mixed.astype(jnp.bfloat16)


def attend(place, queries, states, convs, gains):
    vmem = pl.BlockSpec(memory_space=pltpu.VMEM)
    return pl.pallas_call(
        attend_kernel,
        out_shape=[jax.ShapeDtypeStruct((BLOCK, 2 * VCOLS), jnp.bfloat16)] * 4,
        in_specs=[pl.BlockSpec(memory_space=pltpu.SMEM)] + [vmem] * 8,
        out_specs=[vmem] * 4,
        scratch_shapes=[pltpu.VMEM((ROWS, VCOLS), jnp.float32)],
        compiler_params=pltpu.CompilerParams(vmem_limit_bytes=32 * 1024 * 1024),
    )(place, *queries, *states, *convs, *gains)


def pack_rows(weights, start, count):
    return jnp.concatenate(
        [lax.dynamic_slice_in_dim(w, start, count, axis=0) for w in weights], axis=1
    )


def body(tokens, query_weight, key_weight, value_weight, conv_taps, norm_gain):
    tensor, seq = lax.axis_index("tensor"), lax.axis_index("seq")
    x_at, y_low = tensor // 2, tensor % 2
    core, z_odd = seq % 2, (seq // 2) % 2
    y_at = (seq // 16) * 2 + y_low
    rows = tokens.reshape(BLOCK, tokens.shape[-1])
    weights = (query_weight, key_weight, value_weight)
    half = rows.shape[1] // 2

    one = from_x(rows, 1)
    three = from_x(rows, -1)

    def from_side(array):
        return receive(array, lambda x, y, z, c: (x, y + 2 * c - 1, z, c))

    base = core * half
    sent = [
        pack_rows(weights, base + z_odd * 2 * PIECE, PIECE),
        pack_rows(weights, base + z_odd * 2 * PIECE + PIECE, PIECE),
        pack_rows(weights, base + 4 * PIECE, PIECE),
    ]
    side = [from_side(part) for part in sent]
    low_z = from_z(side[0], -1)
    high_z = from_z(side[1], 1)
    mine = [side[0], side[1], low_z, high_z, side[2]]
    theirs = [from_core(part) for part in mine]
    steps = jnp.stack(
        [z_odd * 2, z_odd * 2 + 1, (1 - z_odd) * 2, (1 - z_odd) * 2 + 1, jnp.full_like(z_odd, 4)]
    )
    offsets = jnp.concatenate([base + steps * PIECE, (half - base) + steps * PIECE]).astype(jnp.int32)

    two_a = from_x(one[: BLOCK // 2], 1)
    two_b = from_x(three[BLOCK // 2 :], -1)

    edges = jnp.concatenate(
        [from_block(rows[BLOCK - 1 :], -1), from_block(rows[:1], 1)], axis=0
    )
    halo = jnp.concatenate(
        [edges, from_x(edges, 1), from_x(edges, 2), from_x(edges, -1), jnp.zeros((8, rows.shape[1]), rows.dtype)],
        axis=0,
    )
    small = jnp.concatenate([conv_taps, norm_gain[None]], axis=0)
    small_other = receive(small, lambda x, y, z, c: (x, y ^ 1, z, c))

    blocks = (rows, one, two_a, two_b, three, halo)
    conv_own, query_own, state_own = project(own_kernel, (), blocks, weights, small)
    conv_other, query_other, state_other = project(
        other_kernel, (offsets,), blocks, (*mine, *theirs), small_other
    )

    same = core == y_low
    keep = jnp.where(same, state_own, state_other)
    give = jnp.where(same, state_other, state_own)
    summed = keep + from_core(give)
    low = summed.astype(jnp.bfloat16)

    def quarter(array, step):
        return lax.dynamic_slice_in_dim(array, ((y_at + step) % NY) * SPLIT, SPLIT, axis=0)

    part = quarter(summed, 0)
    for step in (1, 2, 3):
        part = part + from_y(quarter(low, step), -step).astype(jnp.float32)
    low = part.astype(jnp.bfloat16)
    for step in (1, -1, 2):
        part = part + from_z(low, step).astype(jnp.float32)
    low = part.astype(jnp.bfloat16)
    part = (part + from_z(low, 4).astype(jnp.float32)).astype(jnp.bfloat16)
    ring = [part] + [from_y(part, step) for step in (1, 2, 3)]
    state_mine = lax.dynamic_slice_in_dim(
        jnp.concatenate(ring + ring[:3], axis=0), ((NY - y_at) % NY) * SPLIT, MROWS, axis=0
    )
    state_theirs = from_core(state_mine)
    full_own = jnp.where(same, state_mine, state_theirs)
    full_other = jnp.where(same, state_theirs, state_mine)

    out = attend(
        y_low.reshape(1).astype(jnp.int32),
        (query_own, query_other),
        (full_own, full_other),
        (conv_own, conv_other),
        (small[3:], small_other[3:]),
    )
    back = [out[0], from_x(out[3], 1), from_x(out[2], 2), from_x(out[1], -1)]
    doubled = jnp.stack(back + back[:3], axis=0)
    ordered = lax.dynamic_slice_in_dim(doubled, (NX - x_at) % NX, NX, axis=0)
    result = ordered.transpose(1, 0, 2).reshape(BLOCK, -1)
    return result.reshape(tokens.shape)


def solution(mesh):
    return jax.shard_map(
        body,
        mesh=mesh,
        in_specs=(
            P("seq", "tensor", None),
            P(None, "tensor"),
            P(None, "tensor"),
            P(None, "tensor"),
            P(None, "tensor"),
            P("tensor"),
        ),
        out_specs=P("seq", "tensor", None),
        check_vma=False,
    )
```

time: 453 us -> 181 us (0.40); the launches traced: 447 us -> 180 us
  blocking collectives: 151 us -> 0 us
  waiting for transfers between devices: 216 us -> 77.8 us
  starting transfers between devices: 5.85 us -> 51.5 us
  matrix products: 33.9 us -> 0 us
  Pallas kernels: 0 us -> 30.2 us
  between operations: 13.6 us -> 0.37 us
  other arithmetic: 12.3 us -> 4.27 us
    all_gather x1 -> x0, waiting for transfers between devices: 215 us -> none  [body(): gathered = lax.all_gather(inputs, 'tensor', axis=0, tiled=True)]
    psum x1 -> x0, blocking collectives: 135 us -> none  [body(): lax.psum((state.reshape(-1), total.reshape(-1)), 'seq')]
    ppermute x2 -> x35, waiting for transfers between devices: 0.01 us -> 77.8 us  [the longest x33 52.3 us: receive(): return lax.ppermute(array, AXES, pairs)]
    ppermute x2 -> x35, starting transfers between devices: 5.84 us -> 51.5 us  [the longest x33 46.6 us: receive(): return lax.ppermute(array, AXES, pairs)]
    dot_general x6 -> x0, matrix products: 33.9 us -> none  [the longest x1 13 us: body(): jnp.dot(gathered, value_weight, preferred_element_type=jnp.float32)]
    pallas_call x0 -> x3, Pallas kernels: none -> 30.2 us  [the longest x2 27.3 us: project(): pl.pallas_call(kernel, out_shape=(jax.ShapeDtypeStruct((ROWS, VCOLS), jnp...]
    all_to_all x1 -> x0, blocking collectives: 16.2 us -> none  [body(): lax.all_to_all(mixed, 'tensor', split_axis=0, concat_axis=1, tiled=True)]
    unnamed x14 -> x39, local copies, waits for them, and re-layouts: 1.97 us -> 9.33 us
  transfers between devices with their start and end apart: 3 -> 35, of which waited for: 1 -> 21; matrix products, arithmetic and copies ran while one was open for 3% -> 3% of each run, Pallas kernels for 0% -> 7%
where the time goes in v1:
time: 181 us; the launch traced here: 180 us
  waiting for transfers between devices  77.8 us (43%)
  starting transfers between devices  51.5 us (28%)
  Pallas kernels  30.2 us (17%)
  local copies, waits for them, and re-layouts  16 us (9%)
  other arithmetic  4.27 us (2%)
    ppermute x33, waiting for transfers between devices, receive(): return lax.ppermute(array, AXES, pairs)  52.3 us
    ppermute x33, starting transfers between devices, receive(): return lax.ppermute(array, AXES, pairs)  46.6 us
    pallas_call x2, Pallas kernels, project(): pl.pallas_call(kernel, out_shape=(jax.ShapeDtypeStruct((ROWS, VCOLS), jnp...  27.3 us
    ppermute x2, waiting for transfers between devices, from_block(): return lax.ppermute(array, AXES, pairs)  25.6 us
    unnamed x39, local copies, waits for them, and re-layouts  9.33 us
    ppermute x2, starting transfers between devices, from_block(): return lax.ppermute(array, AXES, pairs)  4.82 us
  transfers between devices with their start and end apart: 35, of which 21 were waited for; matrix products, arithmetic and copies ran while one was open for 3% of the time, Pallas kernels for 7%

profile of v1, /device:TPU:1, one launch (start us, length us, event | category | flops | bytes accessed | tf_op | source)
XLA Modules:
  0.0 180.1 jit_solution(14581622470665816886)
XLA Ops:
  0.0 3.3 %collective-permute-start = (bf16[128,5120]{1,0:T(8,128)(2,1)}, bf16[128,5120]{1,0:T(8,128)(2,1)S(1)}, u32[]{:S(2)}, u32[]{:S(2)}) collective-permute-start(bf16[128,5120]{1,0:T(8,128)(2,1)} %bitcast.24), channel_id=1, source_target_pairs={{64,0},{65,1},{66,2},{67,3},{68,4},{69,5},{70,6},{71,7},{72,8},{73... | collective-permute-start | bytes 3932168 | tf_op jit(solution)/shard_map/ppermute | solution.py:46
  3.3 1.7 constant_dynamic-slice_fusion.4
  6.4 2.8 %collective-permute-start.10 = (bf16[512,896]{1,0:T(8,128)(2,1)S(1)}, bf16[512,896]{1,0:T(8,128)(2,1)}, u32[]{:S(2)}, u32[]{:S(2)}) collective-permute-start(bf16[512,896]{1,0:T(8,128)(2,1)S(1)} %pad_maximum_fusion.1), channel_id=1, source_target_pairs={{48,0},{33,1},{50,2},{35,3},{52,4},{37,5},{54,6},{39,7},{56,8},{41... | collective-permute-start | bytes 2752520 | tf_op jit(solution)/shard_map/ppermute | solution.py:46
  10.8 2.9 %collective-permute-start.4 = (bf16[1,5120]{1,0:T(2,128)(2,1)S(1)}, bf16[1,5120]{1,0:T(2,128)(2,1)S(1)}, u32[]{:S(2)}, u32[]{:S(2)}) collective-permute-start(bf16[1,5120]{1,0:T(2,128)(2,1)S(1)} %get-tuple-element.41), channel_id=1, source_target_pairs={{224,1},{225,2},{226,3},{227,4},{228,5},{229,6},{230,7},{231,8},{2... | collective-permute-start | bytes 30728 | tf_op jit(solution)/shard_map/ppermute | solution.py:72
  13.7 23.0 %collective-permute-done.4 = bf16[1,5120]{1,0:T(2,128)(2,1)S(1)} collective-permute-done((bf16[1,5120]{1,0:T(2,128)(2,1)S(1)}, bf16[1,5120]{1,0:T(2,128)(2,1)S(1)}, u32[]{:S(2)}, u32[]{:S(2)}) %collective-permute-start.4) | collective-permute-done | bytes 10272 | tf_op jit(solution)/shard_map/ppermute | solution.py:72
  36.7 1.9 %collective-permute-start.5 = (bf16[1,5120]{1,0:T(2,128)(2,1)S(1)}, bf16[1,5120]{1,0:T(2,128)(2,1)S(1)}, u32[]{:S(2)}, u32[]{:S(2)}) collective-permute-start(bf16[1,5120]{1,0:T(2,128)(2,1)S(1)} %get-tuple-element.40), channel_id=1, source_target_pairs={{32,0},{33,1},{34,2},{35,3},{36,4},{37,5},{38,6},{39,7},{40,8},{41... | collective-permute-start | bytes 30728 | tf_op jit(solution)/shard_map/ppermute | solution.py:72
  38.6 2.6 %collective-permute-done.5 = bf16[1,5120]{1,0:T(2,128)(2,1)S(1)} collective-permute-done((bf16[1,5120]{1,0:T(2,128)(2,1)S(1)}, bf16[1,5120]{1,0:T(2,128)(2,1)S(1)}, u32[]{:S(2)}, u32[]{:S(2)}) %collective-permute-start.5) | collective-permute-done | bytes 10272 | tf_op jit(solution)/shard_map/ppermute | solution.py:72
  41.3 2.5 %collective-permute-done.19.rest_10_ = f32[4,640]{1,0:T(4,128)S(1)} collective-permute-done((f32[4,640]{1,0:T(4,128)S(1)}, f32[4,640]{1,0:T(4,128)S(1)}, u32[]{:S(2)}, u32[]{:S(2)}) %collective-permute-start.19) | collective-permute-done | bytes 10272 | tf_op jit(solution)/shard_map/ppermute | solution.py:46
  43.8 2.5 %collective-permute-done.6 = bf16[2,5120]{1,0:T(2,128)(2,1)S(1)} collective-permute-done((bf16[2,5120]{1,0:T(2,128)(2,1)S(1)}, bf16[2,5120]{1,0:T(2,128)(2,1)S(1)}, u32[]{:S(2)}, u32[]{:S(2)}) %collective-permute-start.6) | collective-permute-done | bytes 20512 | tf_op jit(solution)/shard_map/ppermute | solution.py:46
  47.6 5.8 %collective-permute-start.12 = (bf16[512,896]{1,0:T(8,128)(2,1)}, bf16[512,896]{1,0:T(8,128)(2,1)}, u32[]{:S(2)}, u32[]{:S(2)}) collective-permute-start(bf16[512,896]{1,0:T(8,128)(2,1)} %collective-permute-done.10.rest_1_), channel_id=1, source_target_pairs={{2,0},{3,1},{4,2},{5,3},{6,4},{7,5},{8,6},{9,7},{10,8},{11,9},{12,... | collective-permute-start | bytes 2752520 | tf_op jit(solution)/shard_map/ppermute | solution.py:46
  53.5 1.8 collective-permute-start.8
  55.4 2.3 %collective-permute-done.7 = bf16[2,5120]{1,0:T(2,128)(2,1)S(1)} collective-permute-done((bf16[2,5120]{1,0:T(2,128)(2,1)S(1)}, bf16[2,5120]{1,0:T(2,128)(2,1)S(1)}, u32[]{:S(2)}, u32[]{:S(2)}) %collective-permute-start.7) | collective-permute-done | bytes 20512 | tf_op jit(solution)/shard_map/ppermute | solution.py:46
  59.1 6.0 %collective-permute-start.15 = (bf16[512,896]{1,0:T(8,128)(2,1)}, bf16[512,896]{1,0:T(8,128)(2,1)}, u32[]{:S(2)}, u32[]{:S(2)}) collective-permute-start(bf16[512,896]{1,0:T(8,128)(2,1)} %collective-permute-done.10.rest_1_), channel_id=1, source_target_pairs={{1,0},{0,1},{3,2},{2,3},{5,4},{4,5},{7,6},{6,7},{9,8},{8,9},{11,10... | collective-permute-start | bytes 2752520 | tf_op jit(solution)/shard_map/ppermute | solution.py:46
  65.1 6.0 %collective-permute-done.12.rest_3_ = bf16[512,896]{1,0:T(8,128)(2,1)} collective-permute-done((bf16[512,896]{1,0:T(8,128)(2,1)}, bf16[512,896]{1,0:T(8,128)(2,1)}, u32[]{:S(2)}, u32[]{:S(2)}) %collective-permute-start.12) | collective-permute-done | bytes 917536 | tf_op jit(solution)/shard_map/ppermute | solution.py:46
  71.1 3.1 %collective-permute-start.14 = (bf16[512,896]{1,0:T(8,128)(2,1)}, bf16[512,896]{1,0:T(8,128)(2,1)}, u32[]{:S(2)}, u32[]{:S(2)}) collective-permute-start(bf16[512,896]{1,0:T(8,128)(2,1)} %collective-permute-done.9.rest_0_), channel_id=1, source_target_pairs={{1,0},{0,1},{3,2},{2,3},{5,4},{4,5},{7,6},{6,7},{9,8},{8,9},{11,10... | collective-permute-start | bytes 2752520 | tf_op jit(solution)/shard_map/ppermute | solution.py:46
  74.3 3.4 %collective-permute-start.18 = (bf16[512,896]{1,0:T(8,128)(2,1)}, bf16[512,896]{1,0:T(8,128)(2,1)}, u32[]{:S(2)}, u32[]{:S(2)}) collective-permute-start(bf16[512,896]{1,0:T(8,128)(2,1)} %collective-permute-done.13.rest_4_), channel_id=1, source_target_pairs={{1,0},{0,1},{3,2},{2,3},{5,4},{4,5},{7,6},{6,7},{9,8},{8,9},{11,10... | collective-permute-start | bytes 2752520 | tf_op jit(solution)/shard_map/ppermute | solution.py:46
  87.7 13.0 %shard_map.64 = (bf16[512,640]{1,0:T(8,128)(2,1)S(1)}, f32[128,512]{1,0:T(8,128)S(1)}, f32[192,640]{1,0:T(8,128)S(1)}) custom-call(bf16[128,5120]{1,0:T(8,128)(2,1)S(1)} %bitcast.26, bf16[128,5120]{1,0:T(8,128)(2,1)S(1)} %collective-permute-done.x1, bf16[64,5120]{1,0:T(8,128)(2,1)S(1)} %copy-done.7, bf16[64,5120]{1,0:T(8,128)(2,1)S(1)} %copy-done.10, ...), custom_call_target="tpu_custom_call" | custom-call | flops 4844421120 | bytes 14581760 | tf_op jit(solution)/shard_map/pallas_call | solution.py:182
  100.8 14.2 %shard_map.65 = (bf16[512,640]{1,0:T(8,128)(2,1)S(1)}, f32[128,512]{1,0:T(8,128)S(1)}, f32[192,640]{1,0:T(8,128)S(1)}) custom-call(s32[10]{0:T(128)S(1)} %pad_add_fusion.offsets, bf16[128,5120]{1,0:T(8,128)(2,1)S(1)} %bitcast.27, bf16[128,5120]{1,0:T(8,128)(2,1)} %copy-done, bf16[64,5120]{1,0:T(8,128)(2,1)S(1)} %copy-done.8, ...), custom_call_target="tpu_custom_call" | custom-call | flops 4844421120 | bytes 14581760 | tf_op jit(solution)/shard_map/pallas_call | solution.py:182
  115.9 2.2 %collective-permute-done.20 = f32[192,640]{1,0:T(8,128)} collective-permute-done((f32[192,640]{1,0:T(8,128)}, f32[192,640]{1,0:T(8,128)}, u32[]{:S(2)}, u32[]{:S(2)}) %collective-permute-start.20) | collective-permute-done | bytes 491552 | tf_op jit(solution)/shard_map/ppermute | solution.py:46
  118.1 1.9 %fusion.2 = (bf16[192,640]{1,0:T(8,128)(2,1)S(1)}, f32[192,640]{1,0:T(8,128)}) fusion(f32[192,640]{1,0:T(8,128)} %collective-permute-done.20, f32[192,640]{1,0:T(8,128)S(1)} %get-tuple-element.17, f32[192,640]{1,0:T(8,128)S(1)} %get-tuple-element.18, pred[]{:T(512)S(6)} %eq.13), kind=kLoop, calls=%fused_computation.47 | loop fusion | flops 368640 | bytes 2211841 | tf_op jit(solution)/shard_map/convert_element_type | solution.py:305
  120.1 2.6 %collective-permute-start.22 = (bf16[48,640]{1,0:T(8,128)(2,1)S(1)}, bf16[48,640]{1,0:T(8,128)(2,1)S(1)}, u32[]{:S(2)}, u32[]{:S(2)}) collective-permute-start(bf16[48,640]{1,0:T(8,128)(2,1)S(1)} %get-tuple-element.46), channel_id=1, source_target_pairs={{16,0},{17,1},{18,2},{19,3},{20,4},{21,5},{22,6},{23,7},{24,8},{25... | collective-permute-start | bytes 184328 | tf_op jit(solution)/shard_map/ppermute | solution.py:46
  130.7 2.0 %collective-permute-done.25 = bf16[48,640]{1,0:T(8,128)(2,1)S(1)} collective-permute-done((bf16[48,640]{1,0:T(8,128)(2,1)S(1)}, bf16[48,640]{1,0:T(8,128)(2,1)S(1)}, u32[]{:S(2)}, u32[]{:S(2)}) %collective-permute-start.25) | collective-permute-done | bytes 61472 | tf_op jit(solution)/shard_map/ppermute | solution.py:46
  134.6 6.3 %collective-permute-done.27 = bf16[48,640]{1,0:T(8,128)(2,1)S(1)} collective-permute-done((bf16[48,640]{1,0:T(8,128)(2,1)S(1)}, bf16[48,640]{1,0:T(8,128)(2,1)S(1)}, u32[]{:S(2)}, u32[]{:S(2)}) %collective-permute-start.27) | collective-permute-done | bytes 61472 | tf_op jit(solution)/shard_map/ppermute | solution.py:46
  140.9 1.9 %collective-permute-start.28 = (bf16[48,640]{1,0:T(8,128)(2,1)S(1)}, bf16[48,640]{1,0:T(8,128)(2,1)S(1)}, u32[]{:S(2)}, u32[]{:S(2)}) collective-permute-start(bf16[48,640]{1,0:T(8,128)(2,1)S(1)} %get-tuple-element.26), channel_id=1, source_target_pairs={{32,0},{33,1},{34,2},{35,3},{36,4},{37,5},{38,6},{39,7},{40,8},{41... | collective-permute-start | bytes 184328 | tf_op jit(solution)/shard_map/ppermute | solution.py:46
  144.3 3.1 %collective-permute-done.29 = bf16[48,640]{1,0:T(8,128)(2,1)S(1)} collective-permute-done((bf16[48,640]{1,0:T(8,128)(2,1)S(1)}, bf16[48,640]{1,0:T(8,128)(2,1)S(1)}, u32[]{:S(2)}, u32[]{:S(2)}) %collective-permute-start.29) | collective-permute-done | bytes 61472 | tf_op jit(solution)/shard_map/ppermute | solution.py:46
  148.2 5.6 %collective-permute-start.31 = (bf16[192,640]{1,0:T(8,128)(2,1)S(1)}, bf16[192,640]{1,0:T(8,128)(2,1)S(1)}, u32[]{:S(2)}, u32[]{:S(2)}) collective-permute-start(bf16[192,640]{1,0:T(8,128)(2,1)S(1)} %constant_dynamic-slice_fusion), channel_id=1, source_target_pairs={{1,0},{0,1},{3,2},{2,3},{5,4},{4,5},{7,6},{6,7},{9,8},{8,9},{11,10... | collective-permute-start | bytes 737288 | tf_op jit(solution)/shard_map/ppermute | solution.py:46
  155.1 2.9 %shard_map.66 = (bf16[128,1280]{1,0:T(8,128)(2,1)S(1)}, bf16[128,1280]{1,0:T(8,128)(2,1)S(1)}, bf16[128,1280]{1,0:T(8,128)(2,1)S(1)}, bf16[128,1280]{1,0:T(8,128)(2,1)S(1)}) custom-call(s32[1]{0:T(128)} %bitcast.place, f32[128,512]{1,0:T(8,128)S(1)} %get-tuple-element.15.query_a, f32[128,512]{1,0:T(8,128)S(1)} %get-tuple-element.16.query_b, ...), custom_call_target="tpu_custom_call" | custom-call | tf_op jit(solution)/shard_map/pallas_call | solution.py:235
  158.0 1.5 collective-permute-start.32
  160.2 6.8 %collective-permute-done.32 = bf16[128,1280]{1,0:T(8,128)(2,1)S(1)} collective-permute-done((bf16[128,1280]{1,0:T(8,128)(2,1)S(1)}, bf16[128,1280]{1,0:T(8,128)(2,1)S(1)}, u32[]{:S(2)}, u32[]{:S(2)}) %collective-permute-start.32) | collective-permute-done | bytes 327712 | tf_op jit(solution)/shard_map/ppermute | solution.py:46
  167.0 2.6 %collective-permute-done.33 = bf16[128,1280]{1,0:T(8,128)(2,1)S(1)} collective-permute-done((bf16[128,1280]{1,0:T(8,128)(2,1)S(1)}, bf16[128,1280]{1,0:T(8,128)(2,1)S(1)}, u32[]{:S(2)}, u32[]{:S(2)}) %collective-permute-start.33) | collective-permute-done | bytes 327712 | tf_op jit(solution)/shard_map/ppermute | solution.py:46
  169.6 8.0 %collective-permute-done.34 = bf16[128,1280]{1,0:T(8,128)(2,1)S(1)} collective-permute-done((bf16[128,1280]{1,0:T(8,128)(2,1)S(1)}, bf16[128,1280]{1,0:T(8,128)(2,1)S(1)}, u32[]{:S(2)}, u32[]{:S(2)}) %collective-permute-start.34) | collective-permute-done | bytes 327712 | tf_op jit(solution)/shard_map/ppermute | solution.py:46
  178.6 1.4 copy.8
  (110 shorter events, 32.1 us)
Async XLA Ops:
  0.0 53.4 %collective-permute-start = (bf16[128,5120]{1,0:T(8,128)(2,1)}, bf16[128,5120]{1,0:T(8,128)(2,1)S(1)}, u32[]{:S(2)}, u32[]{:S(2)}) collective-permute-start(bf16[128,5120]{1,0:T(8,128)(2,1)} %bitcast.24), channel_id=1, source_target_pairs={{64,0},{65,1},{66,2},{67,3},{68,4},{69,5},{70,6},{71,7},{72,8},{73... | collective-permute-start | bytes 3932168 | tf_op jit(solution)/shard_map/ppermute | solution.py:46
  3.3 50.2 %collective-permute-start.2 = (bf16[128,5120]{1,0:T(8,128)(2,1)}, bf16[128,5120]{1,0:T(8,128)(2,1)S(1)}, u32[]{:S(2)}, u32[]{:S(2)}) collective-permute-start(bf16[128,5120]{1,0:T(8,128)(2,1)} %bitcast.25), channel_id=1, source_target_pairs={{192,0},{193,1},{194,2},{195,3},{196,4},{197,5},{198,6},{199,7},{2... | collective-permute-start | bytes 3932168 | tf_op jit(solution)/shard_map/ppermute | solution.py:46
  6.4 41.2 %collective-permute-start.10 = (bf16[512,896]{1,0:T(8,128)(2,1)S(1)}, bf16[512,896]{1,0:T(8,128)(2,1)}, u32[]{:S(2)}, u32[]{:S(2)}) collective-permute-start(bf16[512,896]{1,0:T(8,128)(2,1)S(1)} %pad_maximum_fusion.1), channel_id=1, source_target_pairs={{48,0},{33,1},{50,2},{35,3},{52,4},{37,5},{54,6},{39,7},{56,8},{41... | collective-permute-start | bytes 2752520 | tf_op jit(solution)/shard_map/ppermute | solution.py:46
  9.3 44.1 %collective-permute-start.9 = (bf16[512,896]{1,0:T(8,128)(2,1)S(1)}, bf16[512,896]{1,0:T(8,128)(2,1)}, u32[]{:S(2)}, u32[]{:S(2)}) collective-permute-start(bf16[512,896]{1,0:T(8,128)(2,1)S(1)} %pad_maximum_fusion), channel_id=1, source_target_pairs={{48,0},{33,1},{50,2},{35,3},{52,4},{37,5},{54,6},{39,7},{56,8},{41... | collective-permute-start | bytes 2752520 | tf_op jit(solution)/shard_map/ppermute | solution.py:46
  10.8 25.9 %collective-permute-start.4 = (bf16[1,5120]{1,0:T(2,128)(2,1)S(1)}, bf16[1,5120]{1,0:T(2,128)(2,1)S(1)}, u32[]{:S(2)}, u32[]{:S(2)}) collective-permute-start(bf16[1,5120]{1,0:T(2,128)(2,1)S(1)} %get-tuple-element.41), channel_id=1, source_target_pairs={{224,1},{225,2},{226,3},{227,4},{228,5},{229,6},{230,7},{231,8},{2... | collective-permute-start | bytes 30728 | tf_op jit(solution)/shard_map/ppermute | solution.py:72
  36.7 4.5 %collective-permute-start.5 = (bf16[1,5120]{1,0:T(2,128)(2,1)S(1)}, bf16[1,5120]{1,0:T(2,128)(2,1)S(1)}, u32[]{:S(2)}, u32[]{:S(2)}) collective-permute-start(bf16[1,5120]{1,0:T(2,128)(2,1)S(1)} %get-tuple-element.40), channel_id=1, source_target_pairs={{32,0},{33,1},{34,2},{35,3},{36,4},{37,5},{38,6},{39,7},{40,8},{41... | collective-permute-start | bytes 30728 | tf_op jit(solution)/shard_map/ppermute | solution.py:72
  46.4 12.8 %collective-permute-start.13 = (bf16[512,896]{1,0:T(8,128)(2,1)S(1)}, bf16[512,896]{1,0:T(8,128)(2,1)}, u32[]{:S(2)}, u32[]{:S(2)}) collective-permute-start(bf16[512,896]{1,0:T(8,128)(2,1)S(1)} %pad_maximum_fusion.2), channel_id=1, source_target_pairs={{48,0},{33,1},{50,2},{35,3},{52,4},{37,5},{54,6},{39,7},{56,8},{41... | collective-permute-start | bytes 2752520 | tf_op jit(solution)/shard_map/ppermute | solution.py:46
  47.6 23.5 %collective-permute-start.12 = (bf16[512,896]{1,0:T(8,128)(2,1)}, bf16[512,896]{1,0:T(8,128)(2,1)}, u32[]{:S(2)}, u32[]{:S(2)}) collective-permute-start(bf16[512,896]{1,0:T(8,128)(2,1)} %collective-permute-done.10.rest_1_), channel_id=1, source_target_pairs={{2,0},{3,1},{4,2},{5,3},{6,4},{7,5},{8,6},{9,7},{10,8},{11,9},{12,... | collective-permute-start | bytes 2752520 | tf_op jit(solution)/shard_map/ppermute | solution.py:46
  53.4 20.9 %collective-permute-start.11 = (bf16[512,896]{1,0:T(8,128)(2,1)}, bf16[512,896]{1,0:T(8,128)(2,1)}, u32[]{:S(2)}, u32[]{:S(2)}) collective-permute-start(bf16[512,896]{1,0:T(8,128)(2,1)} %collective-permute-done.9.rest_0_), channel_id=1, source_target_pairs={{14,0},{15,1},{0,2},{1,3},{2,4},{3,5},{4,6},{5,7},{6,8},{7,9},{8,1... | collective-permute-start | bytes 2752520 | tf_op jit(solution)/shard_map/ppermute | solution.py:46
  53.4 4.3 %collective-permute-start.7 = (bf16[2,5120]{1,0:T(2,128)(2,1)S(1)}, bf16[2,5120]{1,0:T(2,128)(2,1)S(1)}, u32[]{:S(2)}, u32[]{:S(2)}) collective-permute-start(bf16[2,5120]{1,0:T(2,128)(2,1)S(1)} %pad_maximum_fusion.3), channel_id=1, source_target_pairs={{128,0},{129,1},{130,2},{131,3},{132,4},{133,5},{134,6},{135,7},{1... | collective-permute-start | bytes 61448 | tf_op jit(solution)/shard_map/ppermute | solution.py:46
  53.5 5.3 %collective-permute-start.8 = (bf16[2,5120]{1,0:T(2,128)(2,1)S(1)}, bf16[2,5120]{1,0:T(2,128)(2,1)S(1)}, u32[]{:S(2)}, u32[]{:S(2)}) collective-permute-start(bf16[2,5120]{1,0:T(2,128)(2,1)S(1)} %pad_maximum_fusion.3), channel_id=1, source_target_pairs={{192,0},{193,1},{194,2},{195,3},{196,4},{197,5},{198,6},{199,7},{2... | collective-permute-start | bytes 61448 | tf_op jit(solution)/shard_map/ppermute | solution.py:46
  57.7 20.0 %collective-permute-start.1 = (bf16[64,5120]{1,0:T(8,128)(2,1)S(1)}, bf16[64,5120]{1,0:T(8,128)(2,1)S(1)}, u32[]{:S(2)}, u32[]{:S(2)}) collective-permute-start(bf16[64,5120]{1,0:T(8,128)(2,1)S(1)} %slice.28), channel_id=1, source_target_pairs={{64,0},{65,1},{66,2},{67,3},{68,4},{69,5},{70,6},{71,7},{72,8},{73... | collective-permute-start | bytes 1966088 | tf_op jit(solution)/shard_map/ppermute | solution.py:46
  58.8 19.7 %collective-permute-start.3 = (bf16[64,5120]{1,0:T(8,128)(2,1)S(1)}, bf16[64,5120]{1,0:T(8,128)(2,1)S(1)}, u32[]{:S(2)}, u32[]{:S(2)}) collective-permute-start(bf16[64,5120]{1,0:T(8,128)(2,1)S(1)} %slice.29), channel_id=1, source_target_pairs={{192,0},{193,1},{194,2},{195,3},{196,4},{197,5},{198,6},{199,7},{2... | collective-permute-start | bytes 1966088 | tf_op jit(solution)/shard_map/ppermute | solution.py:46
  59.1 41.6 %collective-permute-start.15 = (bf16[512,896]{1,0:T(8,128)(2,1)}, bf16[512,896]{1,0:T(8,128)(2,1)}, u32[]{:S(2)}, u32[]{:S(2)}) collective-permute-start(bf16[512,896]{1,0:T(8,128)(2,1)} %collective-permute-done.10.rest_1_), channel_id=1, source_target_pairs={{1,0},{0,1},{3,2},{2,3},{5,4},{4,5},{7,6},{6,7},{9,8},{8,9},{11,10... | collective-permute-start | bytes 2752520 | tf_op jit(solution)/shard_map/ppermute | solution.py:46
  71.1 29.6 %collective-permute-start.14 = (bf16[512,896]{1,0:T(8,128)(2,1)}, bf16[512,896]{1,0:T(8,128)(2,1)}, u32[]{:S(2)}, u32[]{:S(2)}) collective-permute-start(bf16[512,896]{1,0:T(8,128)(2,1)} %collective-permute-done.9.rest_0_), channel_id=1, source_target_pairs={{1,0},{0,1},{3,2},{2,3},{5,4},{4,5},{7,6},{6,7},{9,8},{8,9},{11,10... | collective-permute-start | bytes 2752520 | tf_op jit(solution)/shard_map/ppermute | solution.py:46
  74.3 26.5 %collective-permute-start.18 = (bf16[512,896]{1,0:T(8,128)(2,1)}, bf16[512,896]{1,0:T(8,128)(2,1)}, u32[]{:S(2)}, u32[]{:S(2)}) collective-permute-start(bf16[512,896]{1,0:T(8,128)(2,1)} %collective-permute-done.13.rest_4_), channel_id=1, source_target_pairs={{1,0},{0,1},{3,2},{2,3},{5,4},{4,5},{7,6},{6,7},{9,8},{8,9},{11,10... | collective-permute-start | bytes 2752520 | tf_op jit(solution)/shard_map/ppermute | solution.py:46
  78.5 22.3 %collective-permute-start.17 = (bf16[512,896]{1,0:T(8,128)(2,1)}, bf16[512,896]{1,0:T(8,128)(2,1)}, u32[]{:S(2)}, u32[]{:S(2)}) collective-permute-start(bf16[512,896]{1,0:T(8,128)(2,1)} %collective-permute-done.12.rest_3_), channel_id=1, source_target_pairs={{1,0},{0,1},{3,2},{2,3},{5,4},{4,5},{7,6},{6,7},{9,8},{8,9},{11,10... | collective-permute-start | bytes 2752520 | tf_op jit(solution)/shard_map/ppermute | solution.py:46
  79.4 21.4 %collective-permute-start.16 = (bf16[512,896]{1,0:T(8,128)(2,1)}, bf16[512,896]{1,0:T(8,128)(2,1)}, u32[]{:S(2)}, u32[]{:S(2)}) collective-permute-start(bf16[512,896]{1,0:T(8,128)(2,1)} %collective-permute-done.11.rest_2_), channel_id=1, source_target_pairs={{1,0},{0,1},{3,2},{2,3},{5,4},{4,5},{7,6},{6,7},{9,8},{8,9},{11,10... | collective-permute-start | bytes 2752520 | tf_op jit(solution)/shard_map/ppermute | solution.py:46
  120.0 4.8 %collective-permute-start.21 = (bf16[48,640]{1,0:T(8,128)(2,1)S(1)}, bf16[48,640]{1,0:T(8,128)(2,1)S(1)}, u32[]{:S(2)}, u32[]{:S(2)}) collective-permute-start(bf16[48,640]{1,0:T(8,128)(2,1)S(1)} %get-tuple-element.44), channel_id=1, source_target_pairs={{48,0},{49,1},{50,2},{51,3},{52,4},{53,5},{54,6},{55,7},{56,8},{57... | collective-permute-start | bytes 184328 | tf_op jit(solution)/shard_map/ppermute | solution.py:46
  120.1 5.9 %collective-permute-start.22 = (bf16[48,640]{1,0:T(8,128)(2,1)S(1)}, bf16[48,640]{1,0:T(8,128)(2,1)S(1)}, u32[]{:S(2)}, u32[]{:S(2)}) collective-permute-start(bf16[48,640]{1,0:T(8,128)(2,1)S(1)} %get-tuple-element.46), channel_id=1, source_target_pairs={{16,0},{17,1},{18,2},{19,3},{20,4},{21,5},{22,6},{23,7},{24,8},{25... | collective-permute-start | bytes 184328 | tf_op jit(solution)/shard_map/ppermute | solution.py:46
  122.7 3.9 %collective-permute-start.23 = (bf16[48,640]{1,0:T(8,128)(2,1)S(1)}, bf16[48,640]{1,0:T(8,128)(2,1)S(1)}, u32[]{:S(2)}, u32[]{:S(2)}) collective-permute-start(bf16[48,640]{1,0:T(8,128)(2,1)S(1)} %get-tuple-element.45), channel_id=1, source_target_pairs={{32,0},{33,1},{34,2},{35,3},{36,4},{37,5},{38,6},{39,7},{40,8},{41... | collective-permute-start | bytes 184328 | tf_op jit(solution)/shard_map/ppermute | solution.py:46
  127.5 3.1 %collective-permute-start.24 = (bf16[48,640]{1,0:T(8,128)(2,1)S(1)}, bf16[48,640]{1,0:T(8,128)(2,1)S(1)}, u32[]{:S(2)}, u32[]{:S(2)}) collective-permute-start(bf16[48,640]{1,0:T(8,128)(2,1)S(1)} %get-tuple-element.27), channel_id=1, source_target_pairs={{2,0},{3,1},{4,2},{5,3},{6,4},{7,5},{8,6},{9,7},{10,8},{11,9},{12,... | collective-permute-start | bytes 184328 | tf_op jit(solution)/shard_map/ppermute | solution.py:46
  128.4 4.3 %collective-permute-start.25 = (bf16[48,640]{1,0:T(8,128)(2,1)S(1)}, bf16[48,640]{1,0:T(8,128)(2,1)S(1)}, u32[]{:S(2)}, u32[]{:S(2)}) collective-permute-start(bf16[48,640]{1,0:T(8,128)(2,1)S(1)} %get-tuple-element.27), channel_id=1, source_target_pairs={{14,0},{15,1},{0,2},{1,3},{2,4},{3,5},{4,6},{5,7},{6,8},{7,9},{8,1... | collective-permute-start | bytes 184328 | tf_op jit(solution)/shard_map/ppermute | solution.py:46
  129.1 4.7 %collective-permute-start.26 = (bf16[48,640]{1,0:T(8,128)(2,1)S(1)}, bf16[48,640]{1,0:T(8,128)(2,1)S(1)}, u32[]{:S(2)}, u32[]{:S(2)}) collective-permute-start(bf16[48,640]{1,0:T(8,128)(2,1)S(1)} %get-tuple-element.27), channel_id=1, source_target_pairs={{4,0},{5,1},{6,2},{7,3},{8,4},{9,5},{10,6},{11,7},{12,8},{13,9},{1... | collective-permute-start | bytes 184328 | tf_op jit(solution)/shard_map/ppermute | solution.py:46
  133.8 7.1 %collective-permute-start.27 = (bf16[48,640]{1,0:T(8,128)(2,1)S(1)}, bf16[48,640]{1,0:T(8,128)(2,1)S(1)}, u32[]{:S(2)}, u32[]{:S(2)}) collective-permute-start(bf16[48,640]{1,0:T(8,128)(2,1)S(1)} %fusion), channel_id=1, source_target_pairs={{8,0},{9,1},{10,2},{11,3},{12,4},{13,5},{14,6},{15,7},{0,8},{1,9},... | collective-permute-start | bytes 184328 | tf_op jit(solution)/shard_map/ppermute | solution.py:46
  140.9 3.4 %collective-permute-start.28 = (bf16[48,640]{1,0:T(8,128)(2,1)S(1)}, bf16[48,640]{1,0:T(8,128)(2,1)S(1)}, u32[]{:S(2)}, u32[]{:S(2)}) collective-permute-start(bf16[48,640]{1,0:T(8,128)(2,1)S(1)} %get-tuple-element.26), channel_id=1, source_target_pairs={{32,0},{33,1},{34,2},{35,3},{36,4},{37,5},{38,6},{39,7},{40,8},{41... | collective-permute-start | bytes 184328 | tf_op jit(solution)/shard_map/ppermute | solution.py:46
  142.9 4.6 %collective-permute-start.29 = (bf16[48,640]{1,0:T(8,128)(2,1)S(1)}, bf16[48,640]{1,0:T(8,128)(2,1)S(1)}, u32[]{:S(2)}, u32[]{:S(2)}) collective-permute-start(bf16[48,640]{1,0:T(8,128)(2,1)S(1)} %get-tuple-element.26), channel_id=1, source_target_pairs={{16,0},{17,1},{18,2},{19,3},{20,4},{21,5},{22,6},{23,7},{24,8},{25... | collective-permute-start | bytes 184328 | tf_op jit(solution)/shard_map/ppermute | solution.py:46
  143.6 4.5 %collective-permute-start.30 = (bf16[48,640]{1,0:T(8,128)(2,1)S(1)}, bf16[48,640]{1,0:T(8,128)(2,1)S(1)}, u32[]{:S(2)}, u32[]{:S(2)}) collective-permute-start(bf16[48,640]{1,0:T(8,128)(2,1)S(1)} %get-tuple-element.26), channel_id=1, source_target_pairs={{48,0},{49,1},{50,2},{51,3},{52,4},{53,5},{54,6},{55,7},{56,8},{57... | collective-permute-start | bytes 184328 | tf_op jit(solution)/shard_map/ppermute | solution.py:46
  148.2 6.7 %collective-permute-start.31 = (bf16[192,640]{1,0:T(8,128)(2,1)S(1)}, bf16[192,640]{1,0:T(8,128)(2,1)S(1)}, u32[]{:S(2)}, u32[]{:S(2)}) collective-permute-start(bf16[192,640]{1,0:T(8,128)(2,1)S(1)} %constant_dynamic-slice_fusion), channel_id=1, source_target_pairs={{1,0},{0,1},{3,2},{2,3},{5,4},{4,5},{7,6},{6,7},{9,8},{8,9},{11,10... | collective-permute-start | bytes 737288 | tf_op jit(solution)/shard_map/ppermute | solution.py:46
  158.0 9.0 %collective-permute-start.32 = (bf16[128,1280]{1,0:T(8,128)(2,1)S(1)}, bf16[128,1280]{1,0:T(8,128)(2,1)S(1)}, u32[]{:S(2)}, u32[]{:S(2)}) collective-permute-start(bf16[128,1280]{1,0:T(8,128)(2,1)S(1)} %get-tuple-element.22), channel_id=1, source_target_pairs={{64,0},{65,1},{66,2},{67,3},{68,4},{69,5},{70,6},{71,7},{72,8},{73... | collective-permute-start | bytes 983048 | tf_op jit(solution)/shard_map/ppermute | solution.py:46
  159.5 10.1 %collective-permute-start.33 = (bf16[128,1280]{1,0:T(8,128)(2,1)S(1)}, bf16[128,1280]{1,0:T(8,128)(2,1)S(1)}, u32[]{:S(2)}, u32[]{:S(2)}) collective-permute-start(bf16[128,1280]{1,0:T(8,128)(2,1)S(1)} %get-tuple-element.23), channel_id=1, source_target_pairs={{128,0},{129,1},{130,2},{131,3},{132,4},{133,5},{134,6},{135,7},{1... | collective-permute-start | bytes 983048 | tf_op jit(solution)/shard_map/ppermute | solution.py:46
  160.0 17.6 %collective-permute-start.34 = (bf16[128,1280]{1,0:T(8,128)(2,1)S(1)}, bf16[128,1280]{1,0:T(8,128)(2,1)S(1)}, u32[]{:S(2)}, u32[]{:S(2)}) collective-permute-start(bf16[128,1280]{1,0:T(8,128)(2,1)S(1)} %get-tuple-element.24), channel_id=1, source_target_pairs={{192,0},{193,1},{194,2},{195,3},{196,4},{197,5},{198,6},{199,7},{2... | collective-permute-start | bytes 983048 | tf_op jit(solution)/shard_map/ppermute | solution.py:46
  (17 other events, 156.4 us)

commit v2 on v1

v2 whole, which is shorter than its diff:
```python
import functools

import jax
import jax.numpy as jnp
from jax import lax
from jax.experimental import pallas as pl
from jax.experimental.pallas import tpu as pltpu
from jax.sharding import PartitionSpec as P

FEAT = 16
HEAD_DIM = 80
GROUP = 8
NX, NY, NZ = 4, 4, 8
AXES = ("tensor", "seq")
PIECE = 512
PIECES = (PIECE,) * 10
VMEM_LIMIT = 58 * 1024 * 1024
VMEM_SMALL = 16 * 1024 * 1024
FROWS = 160
MROWS = 192
BLOCK = 128
ROWS = 4 * BLOCK
AHEAD = 3
SLOTS = (0, 1, 3, 2)
VCOLS = GROUP * HEAD_DIM
QCOLS = GROUP * FEAT
GCOLS = VCOLS + 2 * QCOLS
SPLIT = MROWS // NY


def device_of(x, y, z, core):
    x, y, z = x % NX, y % NY, z % NZ
    tensor = x * 2 + (y & 1)
    seq = ((y >> 1) * NZ + z) * 2 + core
    return tensor * 32 + seq


def everywhere():
    return [
        (x, y, z, core)
        for x in range(NX)
        for y in range(NY)
        for z in range(NZ)
        for core in range(2)
    ]


def receive(array, source_of):
    pairs = [(device_of(*source_of(*place)), device_of(*place)) for place in everywhere()]
    return lax.ppermute(array, AXES, pairs)


def from_x(array, step):
    return receive(array, lambda x, y, z, c: (x + step, y, z, c))


def from_y(array, step):
    return receive(array, lambda x, y, z, c: (x, y + step, z, c))


def from_z(array, step):
    return receive(array, lambda x, y, z, c: (x, y, z + step, c))


def from_core(array):
    return receive(array, lambda x, y, z, c: (x, y, z, 1 - c))


def from_far(array):
    place = {}
    for x, y, z, core in everywhere():
        place[x, y & 1, ((y >> 1) * NZ + z) * 2 + core] = device_of(x, y, z, core)
    pairs = []
    for (x, odd, segment), target in place.items():
        source = place.get((x, 1 - odd, segment + (1 if odd else -1)))
        if source is not None:
            pairs.append((source, target))
    return lax.ppermute(array, AXES, pairs)


def features(scaled, off_weight):
    root = 0.5**0.5
    rows = scaled.shape[1]
    parts = [scaled, scaled * scaled * root]
    for step in range(1, FEAT // 2):
        turned = pltpu.roll(scaled, FEAT - step, 0)
        parts.append(scaled * turned * (root * off_weight))
    half = scaled[: FEAT // 2] * scaled[FEAT // 2 :] * (root * off_weight)
    parts.append(half)
    first = lax.broadcasted_iota(jnp.int32, (FEAT // 2, rows), 0) == 0
    parts.append(jnp.where(first, 1.0, 0.0).astype(jnp.float32))
    return jnp.concatenate(parts, axis=0)


def window_of(head):
    start = head * HEAD_DIM // 128 * 128
    stop = -(-(head + 1) * HEAD_DIM // 128) * 128
    return start, stop


def head_mask(head, rows):
    start, stop = window_of(head)
    lane = lax.broadcasted_iota(jnp.int32, (rows, stop - start), 1) + start
    return (lane >= head * HEAD_DIM) & (lane < (head + 1) * HEAD_DIM)


def project_kernel(other, counts, slots, *refs):
    refs = list(refs)
    offsets = refs.pop(0) if other else None
    blocks = [refs.pop(0) for _ in counts]
    weights = [refs.pop(0) for _ in range(len(PIECES) if other else 3)]
    value_out, query_key_out, edge_out, xs, ws, acc, xsem, wsem = refs
    pieces, at = [], 0
    for index, count in enumerate(PIECES):
        start = pl.multiple_of(offsets[index], 256) if other else at
        copies, row = [], 0
        for number, (ref, rows) in enumerate(zip(blocks, counts)):
            copies.append(
                pltpu.make_async_copy(
                    ref.at[:, pl.ds(start, count)],
                    xs.at[pl.ds(row, rows), pl.ds(at, count)],
                    xsem.at[index, number],
                )
            )
            row += rows
        if other:
            copies.append(pltpu.make_async_copy(weights[index], ws.at[pl.ds(at, count)], wsem.at[index, 0]))
        else:
            for kind, (col, width) in enumerate(((0, QCOLS), (QCOLS, QCOLS), (2 * QCOLS, VCOLS))):
                copies.append(
                    pltpu.make_async_copy(
                        weights[kind].at[pl.ds(at, count)],
                        ws.at[pl.ds(at, count), pl.ds(col, width)],
                        wsem.at[index, kind],
                    )
                )
        pieces.append((copies, at, count))
        at += count
    for copies, _, _ in pieces[:AHEAD]:
        for copy in copies:
            copy.start()
    for index, (copies, at, count) in enumerate(pieces):
        for copy in copies:
            copy.wait()
        if index + AHEAD < len(pieces):
            for copy in pieces[index + AHEAD][0]:
                copy.start()
        if index % 2 == 0:
            continue
        span = slice(at - count, at + count)
        part = jnp.dot(xs[:, span], ws[span, :], preferred_element_type=jnp.float32)
        if index == 1:
            acc[...] = part
        else:
            acc[...] += part
    query_key_out[...] = acc[:, : 2 * QCOLS]
    values = acc[:, 2 * QCOLS :].astype(jnp.bfloat16)
    value_out[...] = values
    edge_out[...] = jnp.zeros_like(edge_out)
    for block, slot in enumerate(slots):
        for end, row in ((0, block * BLOCK), (1, block * BLOCK + BLOCK - 1)):
            line = acc[row : row + 1, 2 * QCOLS :].astype(jnp.bfloat16).astype(jnp.float32)
            edge_out[2 * slot + end : 2 * slot + end + 1, :] = line


def project(offsets, blocks, slots, weights):
    counts = tuple(block.shape[0] for block in blocks)
    depth = blocks[0].shape[1]
    rows = sum(counts)
    hbm = pl.BlockSpec(memory_space=pltpu.HBM)
    vmem = pl.BlockSpec(memory_space=pltpu.VMEM)
    scalars = [] if offsets is None else [offsets]
    return pl.pallas_call(
        functools.partial(project_kernel, offsets is not None, counts, slots),
        out_shape=(
            jax.ShapeDtypeStruct((rows, VCOLS), jnp.bfloat16),
            jax.ShapeDtypeStruct((rows, 2 * QCOLS), jnp.float32),
            jax.ShapeDtypeStruct((8, VCOLS), jnp.float32),
        ),
        in_specs=[pl.BlockSpec(memory_space=pltpu.SMEM)] * len(scalars) + [hbm] * (len(blocks) + len(weights)),
        out_specs=(vmem,) * 3,
        scratch_shapes=[
            pltpu.VMEM((rows, depth), jnp.bfloat16),
            pltpu.VMEM((depth, GCOLS), jnp.bfloat16),
            pltpu.VMEM((rows, GCOLS), jnp.float32),
            pltpu.SemaphoreType.DMA((len(PIECES), len(blocks))),
            pltpu.SemaphoreType.DMA((len(PIECES), 3)),
        ],
        compiler_params=pltpu.CompilerParams(vmem_limit_bytes=VMEM_LIMIT),
        cost_estimate=pl.CostEstimate(
            flops=2 * rows * depth * GCOLS, bytes_accessed=2 * depth * (rows + GCOLS), transcendentals=0
        ),
    )(*scalars, *blocks, *weights)


def state_kernel(final, place, values, query_key, near, far, taps, *refs):
    refs = list(refs)
    other_state = refs.pop(0) if final else None
    conv_out, query_out = refs.pop(0), refs.pop(0)
    keep_out, give_out = (refs.pop(0), refs.pop(0)) if final else (None, None)
    state = refs.pop(0)
    x_at, even = place[0], place[1] == 0
    query_out[...] = query_key[:, :QCOLS].T * 0.5
    key = query_key[:, QCOLS:].T * 0.5
    row = lax.broadcasted_iota(jnp.int32, (BLOCK, VCOLS), 0)

    def line(array, block, end):
        at = 2 * (block % 4) + end
        return array[at : at + 1, :]

    for number, block in enumerate(SLOTS):
        span = slice(number * BLOCK, (number + 1) * BLOCK)
        mid = values[span, :].astype(jnp.float32)
        opening = jnp.where((x_at + block) % NX == 0, line(far, block - 1, 1), line(near, block - 1, 1))
        before = jnp.where(even, opening, line(near, block, 1))
        closing = jnp.where((x_at + block) % NX == NX - 1, line(far, block + 1, 0), line(near, block + 1, 0))
        after = jnp.where(even, line(near, block, 0), closing)
        low = jnp.where(row == 0, before, pltpu.roll(mid, 1, 0))
        high = jnp.where(row == BLOCK - 1, after, pltpu.roll(mid, BLOCK - 1, 0))
        conv = taps[0:1, :] * low + taps[1:2, :] * mid + taps[2:3, :] * high
        conv_out[span, :] = conv.astype(jnp.bfloat16)
    state[...] = jnp.zeros_like(state)
    ones = jnp.ones((8, ROWS), jnp.bfloat16)
    for head in range(GROUP):
        feat = features(key[head * FEAT : (head + 1) * FEAT], 1.0).astype(jnp.bfloat16)
        start, stop = window_of(head)
        share = jnp.dot(feat, conv_out[:, start:stop], preferred_element_type=jnp.float32)
        state[:FROWS, start:stop] += jnp.where(head_mask(head, FROWS), share, 0.0)
        total = lax.dot_general(
            ones, feat, (((1,), (1,)), ((), ())), preferred_element_type=jnp.float32
        )
        state[FROWS + head : FROWS + head + 1, :FROWS] = total[0:1]
    if final:
        same = place[2] == 1
        keep_out[...] = jnp.where(same, state[...], other_state[...])
        give_out[...] = jnp.where(same, other_state[...], state[...]).astype(jnp.bfloat16)


def states_of(place, values, query_key, near, far, taps, other_state=None):
    final = other_state is not None
    vmem = pl.BlockSpec(memory_space=pltpu.VMEM)
    state = jax.ShapeDtypeStruct((MROWS, VCOLS), jnp.float32)
    ends = [state, jax.ShapeDtypeStruct((MROWS, VCOLS), jnp.bfloat16)] if final else [state]
    return pl.pallas_call(
        functools.partial(state_kernel, final),
        out_shape=[
            jax.ShapeDtypeStruct((ROWS, VCOLS), jnp.bfloat16),
            jax.ShapeDtypeStruct((QCOLS, ROWS), jnp.float32),
            *ends,
        ],
        in_specs=[pl.BlockSpec(memory_space=pltpu.SMEM)] + [vmem] * (6 if final else 5),
        out_specs=[vmem] * (2 + len(ends)),
        scratch_shapes=[pltpu.VMEM((MROWS, VCOLS), jnp.float32)] if final else [],
        compiler_params=pltpu.CompilerParams(vmem_limit_bytes=VMEM_SMALL),
        cost_estimate=pl.CostEstimate(flops=3 * 10**9, bytes_accessed=4 * 10**6, transcendentals=0),
    )(place, values, query_key, near, far, taps, *([other_state] if final else []))


def pack_kernel(start, query, key, value, *refs):
    outs, sems = refs[:-1], refs[-1]
    copies = []
    for index, out in enumerate(outs):
        count = out.shape[0]
        span = pl.ds(pl.multiple_of(start[index], 256), count)
        for kind, (ref, col, width) in enumerate(
            ((query, 0, QCOLS), (key, QCOLS, QCOLS), (value, 2 * QCOLS, VCOLS))
        ):
            copies.append(
                pltpu.make_async_copy(ref.at[span], out.at[:, pl.ds(col, width)], sems.at[index, kind])
            )
    for copy in copies:
        copy.start()
    for copy in copies:
        copy.wait()


def pack(weights, starts, counts):
    hbm = pl.BlockSpec(memory_space=pltpu.HBM)
    return pl.pallas_call(
        pack_kernel,
        out_shape=[jax.ShapeDtypeStruct((count, GCOLS), jnp.bfloat16) for count in counts],
        in_specs=[pl.BlockSpec(memory_space=pltpu.SMEM)] + [hbm] * 3,
        out_specs=[pl.BlockSpec(memory_space=pltpu.VMEM)] * len(counts),
        scratch_shapes=[pltpu.SemaphoreType.DMA((len(counts), 3))],
        compiler_params=pltpu.CompilerParams(vmem_limit_bytes=VMEM_LIMIT),
    )(jnp.stack(starts).astype(jnp.int32), *weights)


def split_kernel(place, keep, got, part_out, *lows):
    for step in range(NY):
        span = pl.ds(pl.multiple_of((place[0] + step) % NY * SPLIT, SPLIT), SPLIT)
        total = keep[span, :] + got[span, :].astype(jnp.float32)
        if step == 0:
            part_out[...] = total
        else:
            lows[step - 1][...] = total.astype(jnp.bfloat16)


def split(place, keep, got):
    vmem = pl.BlockSpec(memory_space=pltpu.VMEM)
    return pl.pallas_call(
        split_kernel,
        out_shape=[jax.ShapeDtypeStruct((SPLIT, VCOLS), jnp.float32)]
        + [jax.ShapeDtypeStruct((SPLIT, VCOLS), jnp.bfloat16)] * 3,
        in_specs=[pl.BlockSpec(memory_space=pltpu.SMEM), vmem, vmem],
        out_specs=[vmem] * 4,
        compiler_params=pltpu.CompilerParams(vmem_limit_bytes=VMEM_SMALL),
    )(place, keep, got)


def join_kernel(place, *refs):
    blocks, out = refs[:NX], refs[NX]
    width = blocks[0].shape[1]
    for step, block in enumerate(blocks):
        span = pl.ds(pl.multiple_of((place[0] + step) % NX * width, 128), width)
        out[:, span] = block[...]


def join(place, blocks):
    vmem = pl.BlockSpec(memory_space=pltpu.VMEM)
    rows, width = blocks[0].shape
    return pl.pallas_call(
        join_kernel,
        out_shape=jax.ShapeDtypeStruct((rows, NX * width), blocks[0].dtype),
        in_specs=[pl.BlockSpec(memory_space=pltpu.SMEM)] + [vmem] * NX,
        out_specs=vmem,
        compiler_params=pltpu.CompilerParams(vmem_limit_bytes=VMEM_SMALL),
    )(place, *blocks)


def attend_kernel(y_place, same, *refs):
    groups = (refs[0:3], refs[3:6])
    mine, theirs = refs[6:10], refs[10:14]
    outs, acc, states = refs[14:18], refs[18], refs[19]
    for step in range(NY):
        span = pl.ds(pl.multiple_of((y_place[0] + step) % NY * SPLIT, SPLIT), SPLIT)
        states[1 - same[0], span, :] = mine[step][...]
        states[same[0], span, :] = theirs[step][...]
    for number, (query, conv, gain) in enumerate(groups):
        state = states.at[number]
        acc[...] = jnp.zeros_like(acc)
        totals = state[FROWS : FROWS + 16, :FROWS]
        for head in range(GROUP):
            feat = features(query[head * FEAT : (head + 1) * FEAT, :], 2.0)
            denom = jnp.dot(totals, feat.astype(jnp.bfloat16), preferred_element_type=jnp.float32)
            scale = 1.0 / denom[head : head + 1, :]
            scaled = (feat * scale).astype(jnp.bfloat16)
            start, stop = window_of(head)
            part = state[:FROWS, start:stop]
            part = jnp.where(head_mask(head, FROWS), part, jnp.zeros_like(part))
            acc[:, start:stop] += lax.dot_general(
                scaled, part, (((0,), (0,)), ((), ())), preferred_element_type=jnp.float32
            )
        low = y_place[0] % 2
        spot = low if number == 0 else 1 - low
        span = pl.ds(pl.multiple_of(spot * VCOLS, VCOLS), VCOLS)
        for block, slot in enumerate(SLOTS):
            rows = slice(block * BLOCK, (block + 1) * BLOCK)
            mixed = acc[rows, :] * gain[3:4, :] + conv[rows, :].astype(jnp.float32)
            outs[slot][:, span] = mixed.astype(jnp.bfloat16)


def attend(y_place, same, groups, mine, theirs):
    vmem = pl.BlockSpec(memory_space=pltpu.VMEM)
    return pl.pallas_call(
        attend_kernel,
        out_shape=[jax.ShapeDtypeStruct((BLOCK, 2 * VCOLS), jnp.bfloat16)] * 4,
        in_specs=[pl.BlockSpec(memory_space=pltpu.SMEM)] * 2 + [vmem] * 14,
        out_specs=[vmem] * 4,
        scratch_shapes=[
            pltpu.VMEM((ROWS, VCOLS), jnp.float32),
            pltpu.VMEM((2, MROWS, VCOLS), jnp.bfloat16),
        ],
        compiler_params=pltpu.CompilerParams(vmem_limit_bytes=VMEM_SMALL),
    )(y_place, same, *[array for group in groups for array in group], *mine, *theirs)


def body(tokens, query_weight, key_weight, value_weight, conv_taps, norm_gain):
    tensor, seq = lax.axis_index("tensor"), lax.axis_index("seq")
    x_at, y_low = tensor // 2, tensor % 2
    core, z_odd = seq % 2, (seq // 2) % 2
    y_at = (seq // 16) * 2 + y_low
    rows = tokens.reshape(BLOCK, tokens.shape[-1])
    weights = (query_weight, key_weight, value_weight)
    half = rows.shape[1] // 2

    y_place = y_at.reshape(1).astype(jnp.int32)
    x_place = x_at.reshape(1).astype(jnp.int32)
    same = (core == y_low).astype(jnp.int32).reshape(1)
    part = BLOCK // 2

    def from_side(array):
        return receive(array, lambda x, y, z, c: (x, y + 2 * c - 1, z, c))

    def from_other(array):
        return receive(array, lambda x, y, z, c: (x, y ^ 1, z, c))

    one = from_x(rows, 1)
    three = from_x(rows, -1)
    two_top = from_x(one[:part], 1)
    two_low = from_x(three[part:], -1)

    base = core * half
    mixed_z = z_odd * 2 * PIECE
    packed = pack(weights, (base + mixed_z, base + mixed_z + PIECE, base + 4 * PIECE), (PIECE,) * 3)
    side = [from_side(array) for array in packed]
    side_z = [receive(array, lambda x, y, z, c: (x, y, z + 2 * c - 1, c)) for array in side[:2]]
    mine = [side[0], side[1], *side_z, side[2]]
    theirs = [from_core(array) for array in mine]
    flip = 2 * PIECE - mixed_z
    steps = jnp.stack([mixed_z, mixed_z + PIECE, flip, flip + PIECE, jnp.full_like(z_odd, 4 * PIECE)])
    offsets = jnp.concatenate([base + steps, (half - base) + steps]).astype(jnp.int32)
    small = jnp.concatenate([conv_taps, norm_gain[None]], axis=0)
    small_other = from_other(small)

    blocks = (rows, one, three, two_top, two_low)
    place = jnp.concatenate([x_place, y_low.reshape(1).astype(jnp.int32), same])
    values_own, query_key_own, edge_own = project(None, blocks, SLOTS, weights)
    values_other, query_key_other, edge_other = project(offsets, blocks, SLOTS, (*mine, *theirs))
    conv_other, query_other, state_other = states_of(
        place, values_other, query_key_other, from_other(edge_own), from_far(edge_own), small_other
    )
    conv_own, query_own, keep, give = states_of(
        place, values_own, query_key_own, from_other(edge_other), from_far(edge_other), small, state_other
    )

    total, *lows = split(y_place, keep, from_core(give))
    for step, low in zip((1, 2, 3), lows):
        total = total + from_y(low, -step).astype(jnp.float32)
    low = total.astype(jnp.bfloat16)
    for step in (1, -1, 2):
        total = total + from_z(low, step).astype(jnp.float32)
    low = total.astype(jnp.bfloat16)
    quarter = (total + from_z(low, 4).astype(jnp.float32)).astype(jnp.bfloat16)
    mine = [quarter] + [from_y(quarter, step) for step in (1, 2, 3)]
    theirs = [from_core(array) for array in mine]

    out = attend(
        y_place,
        same,
        ((query_own, conv_own, small), (query_other, conv_other, small_other)),
        mine,
        theirs,
    )
    result = join(x_place, [out[0], from_x(out[3], 1), from_x(out[2], 2), from_x(out[1], -1)])
    return result.reshape(tokens.shape)


def solution(mesh):
    return jax.shard_map(
        body,
        mesh=mesh,
        in_specs=(
            P("seq", "tensor", None),
            P(None, "tensor"),
            P(None, "tensor"),
            P(None, "tensor"),
            P(None, "tensor"),
            P("tensor"),
        ),
        out_specs=P("seq", "tensor", None),
        check_vma=False,
    )
```

time: 181 us -> 156 us (0.86)
  waiting for transfers between devices: 77.8 us -> 50.7 us
  starting transfers between devices: 51.5 us -> 66.2 us
  local copies, waits for them, and re-layouts: 16 us -> 4.14 us
  other arithmetic: 4.27 us -> 1.52 us
  Pallas kernels: 30.2 us -> 32.5 us
    ppermute x2, waiting for transfers between devices: 25.6 us -> 0.01 us  [from_far(): return lax.ppermute(array, AXES, pairs)]
    ppermute x33 -> x35, starting transfers between devices: 46.6 us -> 60.7 us  [receive(): return lax.ppermute(array, AXES, pairs)]
    unnamed x39 -> x24, local copies, waits for them, and re-layouts: 9.33 us -> 3.96 us
    dynamic_slice x4 -> x0, local copies, waits for them, and re-layouts: 2.97 us -> none  [the longest x2 2.92 us: pack_rows(): lax.dynamic_slice_in_dim(w, start, count, axis=0)]
    convert_element_type x3, other arithmetic: 2.86 us -> 0.12 us  [the longest x2 0.11 us: body(): low = total.astype(jnp.bfloat16)]
    pallas_call x2 -> x7, Pallas kernels: 27.3 us -> 29.5 us  [the longest x2 20.6 us: project(): pl.pallas_call(functools.partial(project_kernel, offsets is not None, cou...]
    ppermute x33 -> x35, waiting for transfers between devices: 52.3 us -> 50.7 us  [receive(): return lax.ppermute(array, AXES, pairs)]
  transfers between devices with their start and end apart: 35 -> 37, of which waited for: 21 -> 16; matrix products, arithmetic and copies ran while one was open for 3% -> 1% of each run, Pallas kernels for 7% -> 17%
where the time goes in v2:
time: 156 us; the launch traced here: 155 us
  starting transfers between devices  66.2 us (42%)
  waiting for transfers between devices  50.7 us (32%)
  Pallas kernels  32.5 us (21%)
  local copies, waits for them, and re-layouts  4.14 us (3%)
    ppermute x35, starting transfers between devices, receive(): return lax.ppermute(array, AXES, pairs)  60.7 us
    ppermute x35, waiting for transfers between devices, receive(): return lax.ppermute(array, AXES, pairs)  50.7 us
    pallas_call x2, Pallas kernels, project(): pl.pallas_call(functools.partial(project_kernel, offsets is not None, cou...  20.6 us
    ppermute x2, starting transfers between devices, from_far(): return lax.ppermute(array, AXES, pairs)  5.55 us
    pallas_call x1, Pallas kernels, pack(): pl.pallas_call(pack_kernel, out_shape=[jax.ShapeDtypeStruct((count, GCOLS...  4.05 us
    unnamed x24, local copies, waits for them, and re-layouts  3.96 us
    pallas_call x2, Pallas kernels, states_of(): pl.pallas_call(functools.partial(state_kernel, final), out_shape=[jax.Sha...  3.67 us
  transfers between devices with their start and end apart: 37, of which 16 were waited for; matrix products, arithmetic and copies ran while one was open for 1% of the time, Pallas kernels for 17%

profile of v2, /device:TPU:1, one launch (start us, length us, event | category | flops | bytes accessed | tf_op | source)
XLA Modules:
  0.0 155.4 jit_solution(12880169863588942884)
XLA Ops:
  0.0 3.3 %collective-permute-start = (bf16[128,5120]{1,0:T(8,128)(2,1)}, bf16[128,5120]{1,0:T(8,128)(2,1)S(1)}, u32[]{:S(2)}, u32[]{:S(2)}) collective-permute-start(bf16[128,5120]{1,0:T(8,128)(2,1)} %bitcast.13), channel_id=1, source_target_pairs={{64,0},{65,1},{66,2},{67,3},{68,4},{69,5},{70,6},{71,7},{72,8},{73... | collective-permute-start | bytes 3932168 | tf_op jit(solution)/shard_map/ppermute | solution.py:50
  4.0 4.0 %shard_map.65 = (bf16[512,896]{1,0:T(8,128)(2,1)}, bf16[512,896]{1,0:T(8,128)(2,1)}, bf16[512,896]{1,0:T(8,128)(2,1)}) custom-call(s32[3]{0:T(128)} %pad_add_fusion.2.start, bf16[5120,128]{1,0:T(8,128)(2,1)} %query.1, bf16[5120,128]{1,0:T(8,128)(2,1)} %key.1, bf16[5120,640]{1,0:T(8,128)(2,1)} %value.1), custom_call_target="tpu_custom_call" | custom-call | tf_op jit(solution)/shard_map/pallas_call | solution.py:279
  8.0 2.8 %collective-permute-start.4 = (bf16[512,896]{1,0:T(8,128)(2,1)}, bf16[512,896]{1,0:T(8,128)(2,1)}, u32[]{:S(2)}, u32[]{:S(2)}) collective-permute-start(bf16[512,896]{1,0:T(8,128)(2,1)} %get-tuple-element.31), channel_id=1, source_target_pairs={{48,0},{33,1},{50,2},{35,3},{52,4},{37,5},{54,6},{39,7},{56,8},{41... | collective-permute-start | bytes 2752520 | tf_op jit(solution)/shard_map/ppermute | solution.py:50
  11.5 10.0 %collective-permute-done.4.refs_6_ = bf16[512,896]{1,0:T(8,128)(2,1)} collective-permute-done((bf16[512,896]{1,0:T(8,128)(2,1)}, bf16[512,896]{1,0:T(8,128)(2,1)}, u32[]{:S(2)}, u32[]{:S(2)}) %collective-permute-start.4) | collective-permute-done | bytes 917536 | tf_op jit(solution)/shard_map/ppermute | solution.py:50
  21.5 5.6 %collective-permute-start.6 = (bf16[512,896]{1,0:T(8,128)(2,1)}, bf16[512,896]{1,0:T(8,128)(2,1)}, u32[]{:S(2)}, u32[]{:S(2)}) collective-permute-start(bf16[512,896]{1,0:T(8,128)(2,1)} %collective-permute-done.4.refs_6_), channel_id=1, source_target_pairs={{14,0},{3,1},{0,2},{5,3},{2,4},{7,5},{4,6},{9,7},{6,8},{11,9},{8,1... | collective-permute-start | bytes 2752520 | tf_op jit(solution)/shard_map/ppermute | solution.py:50
  27.1 4.3 %collective-permute-done.5.refs_7_ = bf16[512,896]{1,0:T(8,128)(2,1)} collective-permute-done((bf16[512,896]{1,0:T(8,128)(2,1)}, bf16[512,896]{1,0:T(8,128)(2,1)}, u32[]{:S(2)}, u32[]{:S(2)}) %collective-permute-start.5) | collective-permute-done | bytes 917536 | tf_op jit(solution)/shard_map/ppermute | solution.py:50
  31.3 5.6 %collective-permute-start.7 = (bf16[512,896]{1,0:T(8,128)(2,1)}, bf16[512,896]{1,0:T(8,128)(2,1)}, u32[]{:S(2)}, u32[]{:S(2)}) collective-permute-start(bf16[512,896]{1,0:T(8,128)(2,1)} %collective-permute-done.5.refs_7_), channel_id=1, source_target_pairs={{14,0},{3,1},{0,2},{5,3},{2,4},{7,5},{4,6},{9,7},{6,8},{11,9},{8,1... | collective-permute-start | bytes 2752520 | tf_op jit(solution)/shard_map/ppermute | solution.py:50
  36.9 2.8 %collective-permute-start.2 = (bf16[64,5120]{1,0:T(8,128)(2,1)S(1)}, bf16[64,5120]{1,0:T(8,128)(2,1)}, u32[]{:S(2)}, u32[]{:S(2)}) collective-permute-start(bf16[64,5120]{1,0:T(8,128)(2,1)S(1)} %slice.8), channel_id=1, source_target_pairs={{64,0},{65,1},{66,2},{67,3},{68,4},{69,5},{70,6},{71,7},{72,8},{73... | collective-permute-start | bytes 1966088 | tf_op jit(solution)/shard_map/ppermute | solution.py:50
  41.1 3.5 %collective-permute-start.10 = (bf16[512,896]{1,0:T(8,128)(2,1)}, bf16[512,896]{1,0:T(8,128)(2,1)S(1)}, u32[]{:S(2)}, u32[]{:S(2)}) collective-permute-start(bf16[512,896]{1,0:T(8,128)(2,1)} %collective-permute-done.5.refs_7_), channel_id=1, source_target_pairs={{1,0},{0,1},{3,2},{2,3},{5,4},{4,5},{7,6},{6,7},{9,8},{8,9},{11,10... | collective-permute-start | bytes 2752520 | tf_op jit(solution)/shard_map/ppermute | solution.py:50
  44.6 2.9 %collective-permute-done.7.refs_9_ = bf16[512,896]{1,0:T(8,128)(2,1)} collective-permute-done((bf16[512,896]{1,0:T(8,128)(2,1)}, bf16[512,896]{1,0:T(8,128)(2,1)}, u32[]{:S(2)}, u32[]{:S(2)}) %collective-permute-start.7) | collective-permute-done | bytes 917536 | tf_op jit(solution)/shard_map/ppermute | solution.py:50
  47.5 3.8 %collective-permute-start.13 = (bf16[512,896]{1,0:T(8,128)(2,1)}, bf16[512,896]{1,0:T(8,128)(2,1)}, u32[]{:S(2)}, u32[]{:S(2)}) collective-permute-start(bf16[512,896]{1,0:T(8,128)(2,1)} %collective-permute-done.8.refs_10_), channel_id=1, source_target_pairs={{1,0},{0,1},{3,2},{2,3},{5,4},{4,5},{7,6},{6,7},{9,8},{8,9},{11,10... | collective-permute-start | bytes 2752520 | tf_op jit(solution)/shard_map/ppermute | solution.py:50
  51.3 2.5 %collective-permute-done.2.refs_3_.refs_4_ = bf16[64,5120]{1,0:T(8,128)(2,1)} collective-permute-done((bf16[64,5120]{1,0:T(8,128)(2,1)S(1)}, bf16[64,5120]{1,0:T(8,128)(2,1)}, u32[]{:S(2)}, u32[]{:S(2)}) %collective-permute-start.2) | collective-permute-done | bytes 655392 | tf_op jit(solution)/shard_map/ppermute | solution.py:50
  53.9 3.7 %collective-permute-done.3.refs_4_.refs_5_ = bf16[64,5120]{1,0:T(8,128)(2,1)} collective-permute-done((bf16[64,5120]{1,0:T(8,128)(2,1)S(1)}, bf16[64,5120]{1,0:T(8,128)(2,1)}, u32[]{:S(2)}, u32[]{:S(2)}) %collective-permute-start.3) | collective-permute-done | bytes 655392 | tf_op jit(solution)/shard_map/ppermute | solution.py:50
  58.7 9.9 %shard_map.64 = (bf16[512,640]{1,0:T(8,128)(2,1)}, f32[512,256]{1,0:T(8,128)}, f32[8,640]{1,0:T(8,128)}) custom-call(bf16[128,5120]{1,0:T(8,128)(2,1)} %bitcast.15, bf16[128,5120]{1,0:T(8,128)(2,1)} %copy-done.4, bf16[128,5120]{1,0:T(8,128)(2,1)} %copy-done.5, bf16[64,5120]{1,0:T(8,128)(2,1)} %collective-permute-done.2.refs_3_.refs_4_, ...), custom_call_target="tpu_custom_call" | custom-call | flops 4697620480 | bytes 14417920 | tf_op jit(solution)/shard_map/pallas_call | solution.py:173
  70.3 2.4 %collective-permute-start.17 = (f32[8,640]{1,0:T(8,128)}, f32[8,640]{1,0:T(8,128)S(1)}, u32[]{:S(2)}, u32[]{:S(2)}) collective-permute-start(f32[8,640]{1,0:T(8,128)} %get-tuple-element.37), channel_id=1, source_target_pairs={{32,1},{33,2},{34,3},{35,4},{36,5},{37,6},{38,7},{39,8},{40,9},{41... | collective-permute-start | bytes 61448 | tf_op jit(solution)/shard_map/ppermute | solution.py:78
  74.5 10.7 %shard_map.66 = (bf16[512,640]{1,0:T(8,128)(2,1)}, f32[512,256]{1,0:T(8,128)}, f32[8,640]{1,0:T(8,128)}) custom-call(s32[10]{0:T(128)} %pad_add_fusion.1.refs_0_, bf16[128,5120]{1,0:T(8,128)(2,1)} %bitcast.16, bf16[128,5120]{1,0:T(8,128)(2,1)} %copy-done.4, bf16[128,5120]{1,0:T(8,128)(2,1)} %copy-done.5, ...), custom_call_target="tpu_custom_call" | custom-call | flops 4697620480 | bytes 14417920 | tf_op jit(solution)/shard_map/pallas_call | solution.py:173
  85.3 3.1 %collective-permute-start.15 = (f32[8,640]{1,0:T(8,128)}, f32[8,640]{1,0:T(8,128)S(1)}, u32[]{:S(2)}, u32[]{:S(2)}) collective-permute-start(f32[8,640]{1,0:T(8,128)} %get-tuple-element.34), channel_id=1, source_target_pairs={{32,1},{33,2},{34,3},{35,4},{36,5},{37,6},{38,7},{39,8},{40,9},{41... | collective-permute-start | bytes 61448 | tf_op jit(solution)/shard_map/ppermute | solution.py:78
  90.6 1.8 %shard_map.67 = (bf16[512,640]{1,0:T(8,128)(2,1)S(1)}, f32[128,512]{1,0:T(8,128)S(1)}, f32[192,640]{1,0:T(8,128)S(1)}) custom-call(s32[3]{0:T(128)S(1)} %pad_add_fusion.place, bf16[512,640]{1,0:T(8,128)(2,1)S(1)} %copy-done, f32[512,256]{1,0:T(8,128)S(1)} %copy-done.2, f32[8,640]{1,0:T(8,128)S(1)} %collective-permute-done.16.near, ...), custom_call_target="tpu_custom_call" | custom-call | flops 3000000000 | bytes 4000000 | tf_op jit(solution)/shard_map/pallas_call | solution.py:244
  92.5 1.9 %shard_map.68 = (bf16[512,640]{1,0:T(8,128)(2,1)S(1)}, f32[128,512]{1,0:T(8,128)S(1)}, f32[192,640]{1,0:T(8,128)S(1)}, bf16[192,640]{1,0:T(8,128)(2,1)S(1)}) custom-call(s32[3]{0:T(128)S(1)} %pad_add_fusion.place, bf16[512,640]{1,0:T(8,128)(2,1)S(1)} %copy-done.1, f32[512,256]{1,0:T(8,128)S(1)} %copy-done.3, f32[8,640]{1,0:T(8,128)S(1)} %collective-permute-done.14.near, ...), custom_call_target="tpu_custom_call" | custom-call | flops 3000000000 | bytes 4000000 | tf_op jit(solution)/shard_map/pallas_call | solution.py:244
  97.3 3.1 %collective-permute-start.21 = (bf16[48,640]{1,0:T(8,128)(2,1)S(1)}, bf16[48,640]{1,0:T(8,128)(2,1)S(1)}, u32[]{:S(2)}, u32[]{:S(2)}) collective-permute-start(bf16[48,640]{1,0:T(8,128)(2,1)S(1)} %get-tuple-element.47), channel_id=1, source_target_pairs={{16,0},{17,1},{18,2},{19,3},{20,4},{21,5},{22,6},{23,7},{24,8},{25... | collective-permute-start | bytes 184328 | tf_op jit(solution)/shard_map/ppermute | solution.py:50
  100.4 2.0 %collective-permute-start.22 = (bf16[48,640]{1,0:T(8,128)(2,1)S(1)}, bf16[48,640]{1,0:T(8,128)(2,1)S(1)}, u32[]{:S(2)}, u32[]{:S(2)}) collective-permute-start(bf16[48,640]{1,0:T(8,128)(2,1)S(1)} %get-tuple-element.48), channel_id=1, source_target_pairs={{32,0},{33,1},{34,2},{35,3},{36,4},{37,5},{38,6},{39,7},{40,8},{41... | collective-permute-start | bytes 184328 | tf_op jit(solution)/shard_map/ppermute | solution.py:50
  103.8 2.4 %collective-permute-start.23 = (bf16[48,640]{1,0:T(8,128)(2,1)S(1)}, bf16[48,640]{1,0:T(8,128)(2,1)S(1)}, u32[]{:S(2)}, u32[]{:S(2)}) collective-permute-start(bf16[48,640]{1,0:T(8,128)(2,1)S(1)} %fusion), channel_id=1, source_target_pairs={{2,0},{3,1},{4,2},{5,3},{6,4},{7,5},{8,6},{9,7},{10,8},{11,9},{12,... | collective-permute-start | bytes 184328 | tf_op jit(solution)/shard_map/ppermute | solution.py:50
  106.2 2.0 %collective-permute-start.25 = (bf16[48,640]{1,0:T(8,128)(2,1)S(1)}, bf16[48,640]{1,0:T(8,128)(2,1)S(1)}, u32[]{:S(2)}, u32[]{:S(2)}) collective-permute-start(bf16[48,640]{1,0:T(8,128)(2,1)S(1)} %fusion), channel_id=1, source_target_pairs={{4,0},{5,1},{6,2},{7,3},{8,4},{9,5},{10,6},{11,7},{12,8},{13,9},{1... | collective-permute-start | bytes 184328 | tf_op jit(solution)/shard_map/ppermute | solution.py:50
  108.2 2.3 %collective-permute-done.24 = bf16[48,640]{1,0:T(8,128)(2,1)S(1)} collective-permute-done((bf16[48,640]{1,0:T(8,128)(2,1)S(1)}, bf16[48,640]{1,0:T(8,128)(2,1)S(1)}, u32[]{:S(2)}, u32[]{:S(2)}) %collective-permute-start.24) | collective-permute-done | bytes 61472 | tf_op jit(solution)/shard_map/ppermute | solution.py:50
  110.5 4.2 %collective-permute-start.26 = (bf16[48,640]{1,0:T(8,128)(2,1)S(1)}, bf16[48,640]{1,0:T(8,128)(2,1)S(1)}, u32[]{:S(2)}, u32[]{:S(2)}) collective-permute-start(bf16[48,640]{1,0:T(8,128)(2,1)S(1)} %get-tuple-element.53), channel_id=1, source_target_pairs={{8,0},{9,1},{10,2},{11,3},{12,4},{13,5},{14,6},{15,7},{0,8},{1,9},... | collective-permute-start | bytes 184328 | tf_op jit(solution)/shard_map/ppermute | solution.py:50
  114.7 3.0 %collective-permute-done.26 = bf16[48,640]{1,0:T(8,128)(2,1)S(1)} collective-permute-done((bf16[48,640]{1,0:T(8,128)(2,1)S(1)}, bf16[48,640]{1,0:T(8,128)(2,1)S(1)}, u32[]{:S(2)}, u32[]{:S(2)}) %collective-permute-start.26) | collective-permute-done | bytes 61472 | tf_op jit(solution)/shard_map/ppermute | solution.py:50
  117.7 3.0 %collective-permute-start.27 = (bf16[48,640]{1,0:T(8,128)(2,1)S(1)}, bf16[48,640]{1,0:T(8,128)(2,1)S(1)}, u32[]{:S(2)}, u32[]{:S(2)}) collective-permute-start(bf16[48,640]{1,0:T(8,128)(2,1)S(1)} %add_convert_fusion.refs_6_), channel_id=1, source_target_pairs={{32,0},{33,1},{34,2},{35,3},{36,4},{37,5},{38,6},{39,7},{40,8},{41... | collective-permute-start | bytes 184328 | tf_op jit(solution)/shard_map/ppermute | solution.py:50
  121.4 5.1 %collective-permute-start.30 = (bf16[48,640]{1,0:T(8,128)(2,1)S(1)}, bf16[48,640]{1,0:T(8,128)(2,1)S(1)}, u32[]{:S(2)}, u32[]{:S(2)}) collective-permute-start(bf16[48,640]{1,0:T(8,128)(2,1)S(1)} %add_convert_fusion.refs_6_), channel_id=1, source_target_pairs={{1,0},{0,1},{3,2},{2,3},{5,4},{4,5},{7,6},{6,7},{9,8},{8,9},{11,10... | collective-permute-start | bytes 184328 | tf_op jit(solution)/shard_map/ppermute | solution.py:50
  127.3 3.9 %collective-permute-start.32 = (bf16[48,640]{1,0:T(8,128)(2,1)S(1)}, bf16[48,640]{1,0:T(8,128)(2,1)S(1)}, u32[]{:S(2)}, u32[]{:S(2)}) collective-permute-start(bf16[48,640]{1,0:T(8,128)(2,1)S(1)} %collective-permute-done.28.refs_8_), channel_id=1, source_target_pairs={{1,0},{0,1},{3,2},{2,3},{5,4},{4,5},{7,6},{6,7},{9,8},{8,9},{11,10... | collective-permute-start | bytes 184328 | tf_op jit(solution)/shard_map/ppermute | solution.py:50
  132.7 3.0 %shard_map.70 = (bf16[128,1280]{1,0:T(8,128)(2,1)S(1)}, bf16[128,1280]{1,0:T(8,128)(2,1)S(1)}, bf16[128,1280]{1,0:T(8,128)(2,1)S(1)}, bf16[128,1280]{1,0:T(8,128)(2,1)S(1)}) custom-call(s32[1]{0:T(128)} %bitcast.1.place.y_place, s32[1]{0:T(128)} %bitcast.2.same, f32[128,512]{1,0:T(8,128)S(1)} %get-tuple-element.39.refs_0_, ...), custom_call_target="tpu_custom_call" | custom-call | tf_op jit(solution)/shard_map/pallas_call | solution.py:365
  137.2 7.5 %collective-permute-done.34.refs_1_ = bf16[128,1280]{1,0:T(8,128)(2,1)S(1)} collective-permute-done((bf16[128,1280]{1,0:T(8,128)(2,1)S(1)}, bf16[128,1280]{1,0:T(8,128)(2,1)S(1)}, u32[]{:S(2)}, u32[]{:S(2)}) %collective-permute-start.34) | collective-permute-done | bytes 327712 | tf_op jit(solution)/shard_map/ppermute | solution.py:50
  146.2 8.0 %collective-permute-done.36.refs_3_ = bf16[128,1280]{1,0:T(8,128)(2,1)S(1)} collective-permute-done((bf16[128,1280]{1,0:T(8,128)(2,1)S(1)}, bf16[128,1280]{1,0:T(8,128)(2,1)S(1)}, u32[]{:S(2)}, u32[]{:S(2)}) %collective-permute-start.36) | collective-permute-done | bytes 327712 | tf_op jit(solution)/shard_map/ppermute | solution.py:50
  (86 shorter events, 21.2 us)
Async XLA Ops:
  0.0 36.9 %collective-permute-start = (bf16[128,5120]{1,0:T(8,128)(2,1)}, bf16[128,5120]{1,0:T(8,128)(2,1)S(1)}, u32[]{:S(2)}, u32[]{:S(2)}) collective-permute-start(bf16[128,5120]{1,0:T(8,128)(2,1)} %bitcast.13), channel_id=1, source_target_pairs={{64,0},{65,1},{66,2},{67,3},{68,4},{69,5},{70,6},{71,7},{72,8},{73... | collective-permute-start | bytes 3932168 | tf_op jit(solution)/shard_map/ppermute | solution.py:50
  3.3 36.4 %collective-permute-start.1 = (bf16[128,5120]{1,0:T(8,128)(2,1)}, bf16[128,5120]{1,0:T(8,128)(2,1)S(1)}, u32[]{:S(2)}, u32[]{:S(2)}) collective-permute-start(bf16[128,5120]{1,0:T(8,128)(2,1)} %bitcast.14), channel_id=1, source_target_pairs={{192,0},{193,1},{194,2},{195,3},{196,4},{197,5},{198,6},{199,7},{2... | collective-permute-start | bytes 3932168 | tf_op jit(solution)/shard_map/ppermute | solution.py:50
  8.0 13.5 %collective-permute-start.4 = (bf16[512,896]{1,0:T(8,128)(2,1)}, bf16[512,896]{1,0:T(8,128)(2,1)}, u32[]{:S(2)}, u32[]{:S(2)}) collective-permute-start(bf16[512,896]{1,0:T(8,128)(2,1)} %get-tuple-element.31), channel_id=1, source_target_pairs={{48,0},{33,1},{50,2},{35,3},{52,4},{37,5},{54,6},{39,7},{56,8},{41... | collective-permute-start | bytes 2752520 | tf_op jit(solution)/shard_map/ppermute | solution.py:50
  10.8 20.5 %collective-permute-start.5 = (bf16[512,896]{1,0:T(8,128)(2,1)}, bf16[512,896]{1,0:T(8,128)(2,1)}, u32[]{:S(2)}, u32[]{:S(2)}) collective-permute-start(bf16[512,896]{1,0:T(8,128)(2,1)} %get-tuple-element.32), channel_id=1, source_target_pairs={{48,0},{33,1},{50,2},{35,3},{52,4},{37,5},{54,6},{39,7},{56,8},{41... | collective-permute-start | bytes 2752520 | tf_op jit(solution)/shard_map/ppermute | solution.py:50
  11.3 29.8 %collective-permute-start.8 = (bf16[512,896]{1,0:T(8,128)(2,1)}, bf16[512,896]{1,0:T(8,128)(2,1)}, u32[]{:S(2)}, u32[]{:S(2)}) collective-permute-start(bf16[512,896]{1,0:T(8,128)(2,1)} %get-tuple-element.33), channel_id=1, source_target_pairs={{48,0},{33,1},{50,2},{35,3},{52,4},{37,5},{54,6},{39,7},{56,8},{41... | collective-permute-start | bytes 2752520 | tf_op jit(solution)/shard_map/ppermute | solution.py:50
  21.5 23.2 %collective-permute-start.6 = (bf16[512,896]{1,0:T(8,128)(2,1)}, bf16[512,896]{1,0:T(8,128)(2,1)}, u32[]{:S(2)}, u32[]{:S(2)}) collective-permute-start(bf16[512,896]{1,0:T(8,128)(2,1)} %collective-permute-done.4.refs_6_), channel_id=1, source_target_pairs={{14,0},{3,1},{0,2},{5,3},{2,4},{7,5},{4,6},{9,7},{6,8},{11,9},{8,1... | collective-permute-start | bytes 2752520 | tf_op jit(solution)/shard_map/ppermute | solution.py:50
  31.3 16.2 %collective-permute-start.7 = (bf16[512,896]{1,0:T(8,128)(2,1)}, bf16[512,896]{1,0:T(8,128)(2,1)}, u32[]{:S(2)}, u32[]{:S(2)}) collective-permute-start(bf16[512,896]{1,0:T(8,128)(2,1)} %collective-permute-done.5.refs_7_), channel_id=1, source_target_pairs={{14,0},{3,1},{0,2},{5,3},{2,4},{7,5},{4,6},{9,7},{6,8},{11,9},{8,1... | collective-permute-start | bytes 2752520 | tf_op jit(solution)/shard_map/ppermute | solution.py:50
  36.9 16.9 %collective-permute-start.2 = (bf16[64,5120]{1,0:T(8,128)(2,1)S(1)}, bf16[64,5120]{1,0:T(8,128)(2,1)}, u32[]{:S(2)}, u32[]{:S(2)}) collective-permute-start(bf16[64,5120]{1,0:T(8,128)(2,1)S(1)} %slice.8), channel_id=1, source_target_pairs={{64,0},{65,1},{66,2},{67,3},{68,4},{69,5},{70,6},{71,7},{72,8},{73... | collective-permute-start | bytes 1966088 | tf_op jit(solution)/shard_map/ppermute | solution.py:50
  39.8 17.8 %collective-permute-start.3 = (bf16[64,5120]{1,0:T(8,128)(2,1)S(1)}, bf16[64,5120]{1,0:T(8,128)(2,1)}, u32[]{:S(2)}, u32[]{:S(2)}) collective-permute-start(bf16[64,5120]{1,0:T(8,128)(2,1)S(1)} %slice.9), channel_id=1, source_target_pairs={{192,0},{193,1},{194,2},{195,3},{196,4},{197,5},{198,6},{199,7},{2... | collective-permute-start | bytes 1966088 | tf_op jit(solution)/shard_map/ppermute | solution.py:50
  41.1 27.5 %collective-permute-start.10 = (bf16[512,896]{1,0:T(8,128)(2,1)}, bf16[512,896]{1,0:T(8,128)(2,1)S(1)}, u32[]{:S(2)}, u32[]{:S(2)}) collective-permute-start(bf16[512,896]{1,0:T(8,128)(2,1)} %collective-permute-done.5.refs_7_), channel_id=1, source_target_pairs={{1,0},{0,1},{3,2},{2,3},{5,4},{4,5},{7,6},{6,7},{9,8},{8,9},{11,10... | collective-permute-start | bytes 2752520 | tf_op jit(solution)/shard_map/ppermute | solution.py:50
  44.6 25.6 %collective-permute-start.9 = (bf16[512,896]{1,0:T(8,128)(2,1)}, bf16[512,896]{1,0:T(8,128)(2,1)S(1)}, u32[]{:S(2)}, u32[]{:S(2)}) collective-permute-start(bf16[512,896]{1,0:T(8,128)(2,1)} %collective-permute-done.4.refs_6_), channel_id=1, source_target_pairs={{1,0},{0,1},{3,2},{2,3},{5,4},{4,5},{7,6},{6,7},{9,8},{8,9},{11,10... | collective-permute-start | bytes 2752520 | tf_op jit(solution)/shard_map/ppermute | solution.py:50
  47.5 21.2 %collective-permute-start.13 = (bf16[512,896]{1,0:T(8,128)(2,1)}, bf16[512,896]{1,0:T(8,128)(2,1)}, u32[]{:S(2)}, u32[]{:S(2)}) collective-permute-start(bf16[512,896]{1,0:T(8,128)(2,1)} %collective-permute-done.8.refs_10_), channel_id=1, source_target_pairs={{1,0},{0,1},{3,2},{2,3},{5,4},{4,5},{7,6},{6,7},{9,8},{8,9},{11,10... | collective-permute-start | bytes 2752520 | tf_op jit(solution)/shard_map/ppermute | solution.py:50
  53.8 18.8 %collective-permute-start.11 = (bf16[512,896]{1,0:T(8,128)(2,1)}, bf16[512,896]{1,0:T(8,128)(2,1)S(1)}, u32[]{:S(2)}, u32[]{:S(2)}) collective-permute-start(bf16[512,896]{1,0:T(8,128)(2,1)} %collective-permute-done.6.refs_8_), channel_id=1, source_target_pairs={{1,0},{0,1},{3,2},{2,3},{5,4},{4,5},{7,6},{6,7},{9,8},{8,9},{11,10... | collective-permute-start | bytes 2752520 | tf_op jit(solution)/shard_map/ppermute | solution.py:50
  57.6 15.1 %collective-permute-start.12 = (bf16[512,896]{1,0:T(8,128)(2,1)}, bf16[512,896]{1,0:T(8,128)(2,1)S(1)}, u32[]{:S(2)}, u32[]{:S(2)}) collective-permute-start(bf16[512,896]{1,0:T(8,128)(2,1)} %collective-permute-done.7.refs_9_), channel_id=1, source_target_pairs={{1,0},{0,1},{3,2},{2,3},{5,4},{4,5},{7,6},{6,7},{9,8},{8,9},{11,10... | collective-permute-start | bytes 2752520 | tf_op jit(solution)/shard_map/ppermute | solution.py:50
  68.7 19.8 %collective-permute-start.18 = (f32[4,640]{1,0:T(4,128)S(1)}, f32[4,640]{1,0:T(4,128)S(1)}, u32[]{:S(2)}, u32[]{:S(2)}) collective-permute-start(f32[4,640]{1,0:T(4,128)S(1)} %pad_maximum_fusion.taps.refs_2_), channel_id=1, source_target_pairs={{32,0},{33,1},{34,2},{35,3},{36,4},{37,5},{38,6},{39,7},{40,8},{41... | collective-permute-start | bytes 30728 | tf_op jit(solution)/shard_map/ppermute | solution.py:50
  68.8 19.7 %collective-permute-start.16 = (f32[8,640]{1,0:T(8,128)}, f32[8,640]{1,0:T(8,128)S(1)}, u32[]{:S(2)}, u32[]{:S(2)}) collective-permute-start(f32[8,640]{1,0:T(8,128)} %get-tuple-element.37), channel_id=1, source_target_pairs={{32,0},{33,1},{34,2},{35,3},{36,4},{37,5},{38,6},{39,7},{40,8},{41... | collective-permute-start | bytes 61448 | tf_op jit(solution)/shard_map/ppermute | solution.py:50
  70.3 18.3 %collective-permute-start.17 = (f32[8,640]{1,0:T(8,128)}, f32[8,640]{1,0:T(8,128)S(1)}, u32[]{:S(2)}, u32[]{:S(2)}) collective-permute-start(f32[8,640]{1,0:T(8,128)} %get-tuple-element.37), channel_id=1, source_target_pairs={{32,1},{33,2},{34,3},{35,4},{36,5},{37,6},{38,7},{39,8},{40,9},{41... | collective-permute-start | bytes 61448 | tf_op jit(solution)/shard_map/ppermute | solution.py:78
  85.2 7.2 %collective-permute-start.14 = (f32[8,640]{1,0:T(8,128)}, f32[8,640]{1,0:T(8,128)S(1)}, u32[]{:S(2)}, u32[]{:S(2)}) collective-permute-start(f32[8,640]{1,0:T(8,128)} %get-tuple-element.34), channel_id=1, source_target_pairs={{32,0},{33,1},{34,2},{35,3},{36,4},{37,5},{38,6},{39,7},{40,8},{41... | collective-permute-start | bytes 61448 | tf_op jit(solution)/shard_map/ppermute | solution.py:50
  85.3 7.1 %collective-permute-start.15 = (f32[8,640]{1,0:T(8,128)}, f32[8,640]{1,0:T(8,128)S(1)}, u32[]{:S(2)}, u32[]{:S(2)}) collective-permute-start(f32[8,640]{1,0:T(8,128)} %get-tuple-element.34), channel_id=1, source_target_pairs={{32,1},{33,2},{34,3},{35,4},{36,5},{37,6},{38,7},{39,8},{40,9},{41... | collective-permute-start | bytes 61448 | tf_op jit(solution)/shard_map/ppermute | solution.py:78
  96.0 6.3 %collective-permute-start.20 = (bf16[48,640]{1,0:T(8,128)(2,1)S(1)}, bf16[48,640]{1,0:T(8,128)(2,1)S(1)}, u32[]{:S(2)}, u32[]{:S(2)}) collective-permute-start(bf16[48,640]{1,0:T(8,128)(2,1)S(1)} %get-tuple-element.46), channel_id=1, source_target_pairs={{48,0},{49,1},{50,2},{51,3},{52,4},{53,5},{54,6},{55,7},{56,8},{57... | collective-permute-start | bytes 184328 | tf_op jit(solution)/shard_map/ppermute | solution.py:50
  97.3 6.4 %collective-permute-start.21 = (bf16[48,640]{1,0:T(8,128)(2,1)S(1)}, bf16[48,640]{1,0:T(8,128)(2,1)S(1)}, u32[]{:S(2)}, u32[]{:S(2)}) collective-permute-start(bf16[48,640]{1,0:T(8,128)(2,1)S(1)} %get-tuple-element.47), channel_id=1, source_target_pairs={{16,0},{17,1},{18,2},{19,3},{20,4},{21,5},{22,6},{23,7},{24,8},{25... | collective-permute-start | bytes 184328 | tf_op jit(solution)/shard_map/ppermute | solution.py:50
  103.8 4.4 %collective-permute-start.23 = (bf16[48,640]{1,0:T(8,128)(2,1)S(1)}, bf16[48,640]{1,0:T(8,128)(2,1)S(1)}, u32[]{:S(2)}, u32[]{:S(2)}) collective-permute-start(bf16[48,640]{1,0:T(8,128)(2,1)S(1)} %fusion), channel_id=1, source_target_pairs={{2,0},{3,1},{4,2},{5,3},{6,4},{7,5},{8,6},{9,7},{10,8},{11,9},{12,... | collective-permute-start | bytes 184328 | tf_op jit(solution)/shard_map/ppermute | solution.py:50
  110.5 7.2 %collective-permute-start.26 = (bf16[48,640]{1,0:T(8,128)(2,1)S(1)}, bf16[48,640]{1,0:T(8,128)(2,1)S(1)}, u32[]{:S(2)}, u32[]{:S(2)}) collective-permute-start(bf16[48,640]{1,0:T(8,128)(2,1)S(1)} %get-tuple-element.53), channel_id=1, source_target_pairs={{8,0},{9,1},{10,2},{11,3},{12,4},{13,5},{14,6},{15,7},{0,8},{1,9},... | collective-permute-start | bytes 184328 | tf_op jit(solution)/shard_map/ppermute | solution.py:50
  117.7 8.8 %collective-permute-start.27 = (bf16[48,640]{1,0:T(8,128)(2,1)S(1)}, bf16[48,640]{1,0:T(8,128)(2,1)S(1)}, u32[]{:S(2)}, u32[]{:S(2)}) collective-permute-start(bf16[48,640]{1,0:T(8,128)(2,1)S(1)} %add_convert_fusion.refs_6_), channel_id=1, source_target_pairs={{32,0},{33,1},{34,2},{35,3},{36,4},{37,5},{38,6},{39,7},{40,8},{41... | collective-permute-start | bytes 184328 | tf_op jit(solution)/shard_map/ppermute | solution.py:50
  120.7 6.6 %collective-permute-start.28 = (bf16[48,640]{1,0:T(8,128)(2,1)S(1)}, bf16[48,640]{1,0:T(8,128)(2,1)S(1)}, u32[]{:S(2)}, u32[]{:S(2)}) collective-permute-start(bf16[48,640]{1,0:T(8,128)(2,1)S(1)} %add_convert_fusion.refs_6_), channel_id=1, source_target_pairs={{16,0},{17,1},{18,2},{19,3},{20,4},{21,5},{22,6},{23,7},{24,8},{25... | collective-permute-start | bytes 184328 | tf_op jit(solution)/shard_map/ppermute | solution.py:50
  120.7 10.5 %collective-permute-start.29 = (bf16[48,640]{1,0:T(8,128)(2,1)S(1)}, bf16[48,640]{1,0:T(8,128)(2,1)S(1)}, u32[]{:S(2)}, u32[]{:S(2)}) collective-permute-start(bf16[48,640]{1,0:T(8,128)(2,1)S(1)} %add_convert_fusion.refs_6_), channel_id=1, source_target_pairs={{48,0},{49,1},{50,2},{51,3},{52,4},{53,5},{54,6},{55,7},{56,8},{57... | collective-permute-start | bytes 184328 | tf_op jit(solution)/shard_map/ppermute | solution.py:50
  121.4 10.4 %collective-permute-start.30 = (bf16[48,640]{1,0:T(8,128)(2,1)S(1)}, bf16[48,640]{1,0:T(8,128)(2,1)S(1)}, u32[]{:S(2)}, u32[]{:S(2)}) collective-permute-start(bf16[48,640]{1,0:T(8,128)(2,1)S(1)} %add_convert_fusion.refs_6_), channel_id=1, source_target_pairs={{1,0},{0,1},{3,2},{2,3},{5,4},{4,5},{7,6},{6,7},{9,8},{8,9},{11,10... | collective-permute-start | bytes 184328 | tf_op jit(solution)/shard_map/ppermute | solution.py:50
  126.5 5.3 %collective-permute-start.31 = (bf16[48,640]{1,0:T(8,128)(2,1)S(1)}, bf16[48,640]{1,0:T(8,128)(2,1)S(1)}, u32[]{:S(2)}, u32[]{:S(2)}) collective-permute-start(bf16[48,640]{1,0:T(8,128)(2,1)S(1)} %collective-permute-done.27.refs_7_), channel_id=1, source_target_pairs={{1,0},{0,1},{3,2},{2,3},{5,4},{4,5},{7,6},{6,7},{9,8},{8,9},{11,10... | collective-permute-start | bytes 184328 | tf_op jit(solution)/shard_map/ppermute | solution.py:50
  127.3 4.8 %collective-permute-start.32 = (bf16[48,640]{1,0:T(8,128)(2,1)S(1)}, bf16[48,640]{1,0:T(8,128)(2,1)S(1)}, u32[]{:S(2)}, u32[]{:S(2)}) collective-permute-start(bf16[48,640]{1,0:T(8,128)(2,1)S(1)} %collective-permute-done.28.refs_8_), channel_id=1, source_target_pairs={{1,0},{0,1},{3,2},{2,3},{5,4},{4,5},{7,6},{6,7},{9,8},{8,9},{11,10... | collective-permute-start | bytes 184328 | tf_op jit(solution)/shard_map/ppermute | solution.py:50
  135.6 9.0 %collective-permute-start.34 = (bf16[128,1280]{1,0:T(8,128)(2,1)S(1)}, bf16[128,1280]{1,0:T(8,128)(2,1)S(1)}, u32[]{:S(2)}, u32[]{:S(2)}) collective-permute-start(bf16[128,1280]{1,0:T(8,128)(2,1)S(1)} %get-tuple-element.50), channel_id=1, source_target_pairs={{64,0},{65,1},{66,2},{67,3},{68,4},{69,5},{70,6},{71,7},{72,8},{73... | collective-permute-start | bytes 983048 | tf_op jit(solution)/shard_map/ppermute | solution.py:50
  136.1 10.2 %collective-permute-start.35 = (bf16[128,1280]{1,0:T(8,128)(2,1)S(1)}, bf16[128,1280]{1,0:T(8,128)(2,1)S(1)}, u32[]{:S(2)}, u32[]{:S(2)}) collective-permute-start(bf16[128,1280]{1,0:T(8,128)(2,1)S(1)} %get-tuple-element.51), channel_id=1, source_target_pairs={{128,0},{129,1},{130,2},{131,3},{132,4},{133,5},{134,6},{135,7},{1... | collective-permute-start | bytes 983048 | tf_op jit(solution)/shard_map/ppermute | solution.py:50
  136.3 17.9 %collective-permute-start.36 = (bf16[128,1280]{1,0:T(8,128)(2,1)S(1)}, bf16[128,1280]{1,0:T(8,128)(2,1)S(1)}, u32[]{:S(2)}, u32[]{:S(2)}) collective-permute-start(bf16[128,1280]{1,0:T(8,128)(2,1)S(1)} %get-tuple-element.52), channel_id=1, source_target_pairs={{192,0},{193,1},{194,2},{195,3},{196,4},{197,5},{198,6},{199,7},{2... | collective-permute-start | bytes 983048 | tf_op jit(solution)/shard_map/ppermute | solution.py:50
  (17 other events, 126.9 us)

commit v3 on v2

--- a/solution.py
+++ b/solution.py
@@ -20,7 +20,9 @@
 MROWS = 192
 BLOCK = 128
 ROWS = 4 * BLOCK
-AHEAD = 3
+PARTS = (512, 512, 1024, 1024, 1024, 1024)
+AHEAD = 2
+ORDER_COST = 5 * 10**9
 SLOTS = (0, 1, 3, 2)
 VCOLS = GROUP * HEAD_DIM
 QCOLS = GROUP * FEAT
@@ -104,156 +106,184 @@
     return (lane >= head * HEAD_DIM) & (lane < (head + 1) * HEAD_DIM)
 
 
-def project_kernel(other, counts, slots, *refs):
+def project_kernel(counts, offsets, *refs):
     refs = list(refs)
-    offsets = refs.pop(0) if other else None
     blocks = [refs.pop(0) for _ in counts]
-    weights = [refs.pop(0) for _ in range(len(PIECES) if other else 3)]
-    value_out, query_key_out, edge_out, xs, ws, acc, xsem, wsem = refs
-    pieces, at = [], 0
-    for index, count in enumerate(PIECES):
-        start = pl.multiple_of(offsets[index], 256) if other else at
+    weights = [refs.pop(0) for _ in range(3)]
+    pieces = [refs.pop(0) for _ in PIECES]
+    refs.pop(0)
+    value_outs, query_key_outs, edge_out = refs[0:2], refs[2:4], refs[4]
+    xs, ws, acc, xsem, wsem, psem = refs[5:]
+    stages, at = [], 0
+    for index, count in enumerate(PARTS):
         copies, row = [], 0
         for number, (ref, rows) in enumerate(zip(blocks, counts)):
             copies.append(
                 pltpu.make_async_copy(
-                    ref.at[:, pl.ds(start, count)],
+                    ref.at[:, pl.ds(at, count)],
                     xs.at[pl.ds(row, rows), pl.ds(at, count)],
                     xsem.at[index, number],
                 )
             )
             row += rows
-        if other:
-            copies.append(pltpu.make_async_copy(weights[index], ws.at[pl.ds(at, count)], wsem.at[index, 0]))
-        else:
-            for kind, (col, width) in enumerate(((0, QCOLS), (QCOLS, QCOLS), (2 * QCOLS, VCOLS))):
-                copies.append(
-                    pltpu.make_async_copy(
-                        weights[kind].at[pl.ds(at, count)],
-                        ws.at[pl.ds(at, count), pl.ds(col, width)],
-                        wsem.at[index, kind],
-                    )
+        for kind, (col, width) in enumerate(((0, QCOLS), (QCOLS, QCOLS), (2 * QCOLS, VCOLS))):
+            copies.append(
+                pltpu.make_async_copy(
+                    weights[kind].at[pl.ds(at, count)],
+                    ws.at[0, pl.ds(at, count), pl.ds(col, width)],
+                    wsem.at[index, kind],
                 )
-        pieces.append((copies, at, count))
+            )
+        stages.append((0, copies, at, at, count))
         at += count
-    for copies, _, _ in pieces[:AHEAD]:
-        for copy in copies:
+    at = 0
+    for index, members in enumerate(((0, 1), (2, 3), (4,), (5, 6), (7, 8), (9,))):
+        copies = [
+            pltpu.make_async_copy(
+                pieces[member], ws.at[1, pl.ds(at + step * PIECE, PIECE)], psem.at[member]
+            )
+            for step, member in enumerate(members)
+        ]
+        count = len(members) * PIECE
+        stages.append((1, copies, at, pl.multiple_of(offsets[members[0]], PIECE), count))
+        at += count
+
+    for stage in stages[:AHEAD]:
+        for copy in stage[1]:
             copy.start()
-    for index, (copies, at, count) in enumerate(pieces):
+    for index, (group, copies, at, start, count) in enumerate(stages):
         for copy in copies:
             copy.wait()
-        if index + AHEAD < len(pieces):
-            for copy in pieces[index + AHEAD][0]:
+        if index + AHEAD < len(stages):
+            for copy in stages[index + AHEAD][1]:
                 copy.start()
-        if index % 2 == 0:
-            continue
-        span = slice(at - count, at + count)
-        part = jnp.dot(xs[:, span], ws[span, :], preferred_element_type=jnp.float32)
-        if index == 1:
+        part = jnp.dot(
+            xs[:, pl.ds(start, count)], ws[group, at : at + count, :], preferred_element_type=jnp.float32
+        )
+        if at == 0:
             acc[...] = part
         else:
             acc[...] += part
-    query_key_out[...] = acc[:, : 2 * QCOLS]
-    values = acc[:, 2 * QCOLS :].astype(jnp.bfloat16)
-    value_out[...] = values
-    edge_out[...] = jnp.zeros_like(edge_out)
-    for block, slot in enumerate(slots):
-        for end, row in ((0, block * BLOCK), (1, block * BLOCK + BLOCK - 1)):
-            line = acc[row : row + 1, 2 * QCOLS :].astype(jnp.bfloat16).astype(jnp.float32)
-            edge_out[2 * slot + end : 2 * slot + end + 1, :] = line
-
-
-def project(offsets, blocks, slots, weights):
+        if index + 1 < len(stages) and stages[index + 1][0] == group:
+            continue
+        query_key_outs[group][...] = acc[:, : 2 * QCOLS]
+        value_outs[group][...] = acc[:, 2 * QCOLS :].astype(jnp.bfloat16)
+        for block, slot in enumerate(SLOTS):
+            for end, row in ((0, block * BLOCK), (1, block * BLOCK + BLOCK - 1)):
+                line = acc[row : row + 1, 2 * QCOLS :].astype(jnp.bfloat16).astype(jnp.float32)
+                edge_out[8 * group + 2 * slot + end : 8 * group + 2 * slot + end + 1, :] = line
+
+
+def project(offsets, blocks, weights, pieces, after):
     counts = tuple(block.shape[0] for block in blocks)
     depth = blocks[0].shape[1]
-    rows = sum(counts)
     hbm = pl.BlockSpec(memory_space=pltpu.HBM)
     vmem = pl.BlockSpec(memory_space=pltpu.VMEM)
-    scalars = [] if offsets is None else [offsets]
-    return pl.pallas_call(
-        functools.partial(project_kernel, offsets is not None, counts, slots),
-        out_shape=(
-            jax.ShapeDtypeStruct((rows, VCOLS), jnp.bfloat16),
-            jax.ShapeDtypeStruct((rows, 2 * QCOLS), jnp.float32),
-            jax.ShapeDtypeStruct((8, VCOLS), jnp.float32),
-        ),
-        in_specs=[pl.BlockSpec(memory_space=pltpu.SMEM)] * len(scalars) + [hbm] * (len(blocks) + len(weights)),
-        out_specs=(vmem,) * 3,
+    return pl.pallas_call(
+        functools.partial(project_kernel, counts),
+        out_shape=[jax.ShapeDtypeStruct((ROWS, VCOLS), jnp.bfloat16)] * 2
+        + [jax.ShapeDtypeStruct((ROWS, 2 * QCOLS), jnp.float32)] * 2
+        + [jax.ShapeDtypeStruct((16, VCOLS), jnp.float32)],
+        in_specs=[pl.BlockSpec(memory_space=pltpu.SMEM)] + [hbm] * (len(blocks) + 4 + len(pieces)),
+        out_specs=[vmem] * 5,
         scratch_shapes=[
-            pltpu.VMEM((rows, depth), jnp.bfloat16),
-            pltpu.VMEM((depth, GCOLS), jnp.bfloat16),
-            pltpu.VMEM((rows, GCOLS), jnp.float32),
-            pltpu.SemaphoreType.DMA((len(PIECES), len(blocks))),
-            pltpu.SemaphoreType.DMA((len(PIECES), 3)),
+            pltpu.VMEM((ROWS, depth), jnp.bfloat16),
+            pltpu.VMEM((2, depth, GCOLS), jnp.bfloat16),
+            pltpu.VMEM((ROWS, GCOLS), jnp.float32),
+            pltpu.SemaphoreType.DMA((len(PARTS), len(blocks))),
+            pltpu.SemaphoreType.DMA((len(PARTS), 3)),
+            pltpu.SemaphoreType.DMA((len(pieces),)),
         ],
         compiler_params=pltpu.CompilerParams(vmem_limit_bytes=VMEM_LIMIT),
         cost_estimate=pl.CostEstimate(
-            flops=2 * rows * depth * GCOLS, bytes_accessed=2 * depth * (rows + GCOLS), transcendentals=0
+            flops=4 * ROWS * depth * GCOLS, bytes_accessed=2 * depth * (ROWS + 2 * GCOLS), transcendentals=0
         ),
-    )(*scalars, *blocks, *weights)
-
-
-def state_kernel(final, place, values, query_key, near, far, taps, *refs):
-    refs = list(refs)
-    other_state = refs.pop(0) if final else None
-    conv_out, query_out = refs.pop(0), refs.pop(0)
-    keep_out, give_out = (refs.pop(0), refs.pop(0)) if final else (None, None)
-    state = refs.pop(0)
+    )(offsets, *blocks, *weights, *pieces, after)
+
+
+def order_kernel(top, low, out, scratch, sems):
+    copies = [
+        pltpu.make_async_copy(ref.at[pl.ds(0, 16), pl.ds(0, 128)], scratch.at[number], sems.at[number])
+        for number, ref in enumerate((top, low))
+    ]
+    for copy in copies:
+        copy.start()
+    for copy in copies:
+        copy.wait()
+    out[...] = scratch[0] + scratch[1]
+
+
+def arrived(top, low):
+    hbm = pl.BlockSpec(memory_space=pltpu.HBM)
+    return pl.pallas_call(
+        order_kernel,
+        out_shape=jax.ShapeDtypeStruct((16, 128), top.dtype),
+        in_specs=[hbm, hbm],
+        out_specs=pl.BlockSpec(memory_space=pltpu.VMEM),
+        scratch_shapes=[pltpu.VMEM((2, 16, 128), top.dtype), pltpu.SemaphoreType.DMA((2,))],
+        compiler_params=pltpu.CompilerParams(vmem_limit_bytes=VMEM_LIMIT),
+        cost_estimate=pl.CostEstimate(flops=ORDER_COST, bytes_accessed=15 * 10**6, transcendentals=0),
+    )(top, low)
+
+
+def state_kernel(place, *refs):
+    values, query_keys, (near, far), taps = refs[0:2], refs[2:4], refs[4:6], refs[6:8]
+    convs, queries, (keep_out, give_out), states = refs[8:10], refs[10:12], refs[12:14], refs[14]
     x_at, even = place[0], place[1] == 0
-    query_out[...] = query_key[:, :QCOLS].T * 0.5
-    key = query_key[:, QCOLS:].T * 0.5
     row = lax.broadcasted_iota(jnp.int32, (BLOCK, VCOLS), 0)
-
-    def line(array, block, end):
-        at = 2 * (block % 4) + end
-        return array[at : at + 1, :]
-
-    for number, block in enumerate(SLOTS):
-        span = slice(number * BLOCK, (number + 1) * BLOCK)
-        mid = values[span, :].astype(jnp.float32)
-        opening = jnp.where((x_at + block) % NX == 0, line(far, block - 1, 1), line(near, block - 1, 1))
-        before = jnp.where(even, opening, line(near, block, 1))
-        closing = jnp.where((x_at + block) % NX == NX - 1, line(far, block + 1, 0), line(near, block + 1, 0))
-        after = jnp.where(even, line(near, block, 0), closing)
-        low = jnp.where(row == 0, before, pltpu.roll(mid, 1, 0))
-        high = jnp.where(row == BLOCK - 1, after, pltpu.roll(mid, BLOCK - 1, 0))
-        conv = taps[0:1, :] * low + taps[1:2, :] * mid + taps[2:3, :] * high
-        conv_out[span, :] = conv.astype(jnp.bfloat16)
-    state[...] = jnp.zeros_like(state)
     ones = jnp.ones((8, ROWS), jnp.bfloat16)
-    for head in range(GROUP):
-        feat = features(key[head * FEAT : (head + 1) * FEAT], 1.0).astype(jnp.bfloat16)
-        start, stop = window_of(head)
-        share = jnp.dot(feat, conv_out[:, start:stop], preferred_element_type=jnp.float32)
-        state[:FROWS, start:stop] += jnp.where(head_mask(head, FROWS), share, 0.0)
-        total = lax.dot_general(
-            ones, feat, (((1,), (1,)), ((), ())), preferred_element_type=jnp.float32
-        )
-        state[FROWS + head : FROWS + head + 1, :FROWS] = total[0:1]
-    if final:
-        same = place[2] == 1
-        keep_out[...] = jnp.where(same, state[...], other_state[...])
-        give_out[...] = jnp.where(same, other_state[...], state[...]).astype(jnp.bfloat16)
-
-
-def states_of(place, values, query_key, near, far, taps, other_state=None):
-    final = other_state is not None
+    states[...] = jnp.zeros_like(states)
+    for group in range(2):
+        state, conv_out = states.at[group], convs[group]
+        queries[group][...] = query_keys[group][:, :QCOLS].T * 0.5
+        key = query_keys[group][:, QCOLS:].T * 0.5
+
+        def line(ref, block, end):
+            at = 8 * (1 - group) + 2 * (block % 4) + end
+            return ref[at : at + 1, :]
+
+        for number, block in enumerate(SLOTS):
+            span = slice(number * BLOCK, (number + 1) * BLOCK)
+            mid = values[group][span, :].astype(jnp.float32)
+            opening = jnp.where((x_at + block) % NX == 0, line(far, block - 1, 1), line(near, block - 1, 1))
+            before = jnp.where(even, opening, line(near, block, 1))
+            closing = jnp.where((x_at + block) % NX == NX - 1, line(far, block + 1, 0), line(near, block + 1, 0))
+            after = jnp.where(even, line(near, block, 0), closing)
+            low = jnp.where(row == 0, before, pltpu.roll(mid, 1, 0))
+            high = jnp.where(row == BLOCK - 1, after, pltpu.roll(mid, BLOCK - 1, 0))
+            tap = taps[group]
+            conv = tap[0:1, :] * low + tap[1:2, :] * mid + tap[2:3, :] * high
+            conv_out[span, :] = conv.astype(jnp.bfloat16)
+        for head in range(GROUP):
+            feat = features(key[head * FEAT : (head + 1) * FEAT], 1.0).astype(jnp.bfloat16)
+            start, stop = window_of(head)
+            share = jnp.dot(feat, conv_out[:, start:stop], preferred_element_type=jnp.float32)
+            state[:FROWS, start:stop] += jnp.where(head_mask(head, FROWS), share, 0.0)
+            total = lax.dot_general(
+                ones, feat, (((1,), (1,)), ((), ())), preferred_element_type=jnp.float32
+            )
+            state[FROWS + head : FROWS + head + 1, :FROWS] = total[0:1]
+    same = place[2] == 1
+    keep_out[...] = jnp.where(same, states[0], states[1])
+    give_out[...] = jnp.where(same, states[1], states[0]).astype(jnp.bfloat16)
+
+
+def states_of(place, values, query_keys, near, far, taps):
     vmem = pl.BlockSpec(memory_space=pltpu.VMEM)
-    state = jax.ShapeDtypeStruct((MROWS, VCOLS), jnp.float32)
-    ends = [state, jax.ShapeDtypeStruct((MROWS, VCOLS), jnp.bfloat16)] if final else [state]
-    return pl.pallas_call(
-        functools.partial(state_kernel, final),
-        out_shape=[
-            jax.ShapeDtypeStruct((ROWS, VCOLS), jnp.bfloat16),
-            jax.ShapeDtypeStruct((QCOLS, ROWS), jnp.float32),
-            *ends,
+    return pl.pallas_call(
+        state_kernel,
+        out_shape=[jax.ShapeDtypeStruct((ROWS, VCOLS), jnp.bfloat16)] * 2
+        + [jax.ShapeDtypeStruct((QCOLS, ROWS), jnp.float32)] * 2
+        + [
+            jax.ShapeDtypeStruct((MROWS, VCOLS), jnp.float32),
+            jax.ShapeDtypeStruct((MROWS, VCOLS), jnp.bfloat16),
         ],
-        in_specs=[pl.BlockSpec(memory_space=pltpu.SMEM)] + [vmem] * (6 if final else 5),
-        out_specs=[vmem] * (2 + len(ends)),
-        scratch_shapes=[pltpu.VMEM((MROWS, VCOLS), jnp.float32)] if final else [],
+        in_specs=[pl.BlockSpec(memory_space=pltpu.SMEM)] + [vmem] * 8,
+        out_specs=[vmem] * 6,
+        scratch_shapes=[pltpu.VMEM((2, MROWS, VCOLS), jnp.float32)],
         compiler_params=pltpu.CompilerParams(vmem_limit_bytes=VMEM_SMALL),
-        cost_estimate=pl.CostEstimate(flops=3 * 10**9, bytes_accessed=4 * 10**6, transcendentals=0),
-    )(place, values, query_key, near, far, taps, *([other_state] if final else []))
+        cost_estimate=pl.CostEstimate(flops=6 * 10**9, bytes_accessed=8 * 10**6, transcendentals=0),
+    )(place, *values, *query_keys, near, far, *taps)
 
 
 def pack_kernel(start, query, key, value, *refs):
@@ -415,13 +445,16 @@
 
     blocks = (rows, one, three, two_top, two_low)
     place = jnp.concatenate([x_place, y_low.reshape(1).astype(jnp.int32), same])
-    values_own, query_key_own, edge_own = project(None, blocks, SLOTS, weights)
-    values_other, query_key_other, edge_other = project(offsets, blocks, SLOTS, (*mine, *theirs))
-    conv_other, query_other, state_other = states_of(
-        place, values_other, query_key_other, from_other(edge_own), from_far(edge_own), small_other
+    value_own, value_other, query_key_own, query_key_other, edge = project(
+        offsets, blocks, weights, (*mine, *theirs), arrived(two_top, two_low)
     )
-    conv_own, query_own, keep, give = states_of(
-        place, values_own, query_key_own, from_other(edge_other), from_far(edge_other), small, state_other
+    conv_own, conv_other, query_own, query_other, keep, give = states_of(
+        place,
+        (value_own, value_other),
+        (query_key_own, query_key_other),
+        from_other(edge),
+        from_far(edge),
+        (small, small_other),
     )
 
     total, *lows = split(y_place, keep, from_core(give))

time: 156 us -> 152 us (0.974)
  starting transfers between devices: 66.2 us -> 59 us
  waiting for transfers between devices: 50.7 us -> 57.4 us
  Pallas kernels: 32.5 us -> 28.6 us
    ppermute x35 -> x34, starting transfers between devices: 60.7 us -> 56.5 us  [receive(): return lax.ppermute(array, AXES, pairs)]
    pallas_call x4 -> x3, Pallas kernels: 24.3 us -> 20.4 us  [the longest x1 16.1 us: project(): pl.pallas_call(functools.partial(project_kernel, counts), out_shape=[jax....]
    ppermute x35 -> x34, waiting for transfers between devices: 50.7 us -> 54.4 us  [receive(): return lax.ppermute(array, AXES, pairs)]
    ppermute x2 -> x1, starting transfers between devices: 5.55 us -> 2.46 us  [from_far(): return lax.ppermute(array, AXES, pairs)]
    ppermute x2 -> x1, waiting for transfers between devices: 0.01 us -> 2.97 us  [from_far(): return lax.ppermute(array, AXES, pairs)]
    unnamed x24 -> x18, local copies, waits for them, and re-layouts: 3.96 us -> 5.19 us
  transfers between devices with their start and end apart: 37 -> 35, of which waited for: 16 -> 18; matrix products, arithmetic and copies ran while one was open for 1% -> 1% of each run, Pallas kernels for 17% -> 14%
where the time goes in v3:
time: 152 us
  starting transfers between devices  59 us (39%)
  waiting for transfers between devices  57.4 us (38%)
  Pallas kernels  28.6 us (19%)
  local copies, waits for them, and re-layouts  5.36 us (4%)
    ppermute x34, starting transfers between devices, receive(): return lax.ppermute(array, AXES, pairs)  56.5 us
    ppermute x34, waiting for transfers between devices, receive(): return lax.ppermute(array, AXES, pairs)  54.4 us
    pallas_call x1, Pallas kernels, project(): pl.pallas_call(functools.partial(project_kernel, counts), out_shape=[jax....  16.1 us
    unnamed x18, local copies, waits for them, and re-layouts  5.19 us
    pallas_call x1, Pallas kernels, pack(): pl.pallas_call(pack_kernel, out_shape=[jax.ShapeDtypeStruct((count, GCOLS...  4.06 us
  transfers between devices with their start and end apart: 35, of which 18 were waited for; matrix products, arithmetic and copies ran while one was open for 1% of the time, Pallas kernels for 14%

profile of v3, /device:TPU:1, one launch (start us, length us, event | category | flops | bytes accessed | tf_op | source)
XLA Modules:
  0.0 152.0 jit_solution(14957992172749709311)
XLA Ops:
  0.0 3.3 %collective-permute-start = (bf16[128,5120]{1,0:T(8,128)(2,1)}, bf16[128,5120]{1,0:T(8,128)(2,1)S(1)}, u32[]{:S(2)}, u32[]{:S(2)}) collective-permute-start(bf16[128,5120]{1,0:T(8,128)(2,1)} %bitcast.13), channel_id=1, source_target_pairs={{64,0},{65,1},{66,2},{67,3},{68,4},{69,5},{70,6},{71,7},{72,8},{73... | collective-permute-start | bytes 3932168 | tf_op jit(solution)/shard_map/ppermute | solution.py:52
  3.9 4.1 %shard_map.64 = (bf16[512,896]{1,0:T(8,128)(2,1)}, bf16[512,896]{1,0:T(8,128)(2,1)}, bf16[512,896]{1,0:T(8,128)(2,1)}) custom-call(s32[3]{0:T(128)} %pad_add_fusion.2.start, bf16[5120,128]{1,0:T(8,128)(2,1)} %refs_5_.1, bf16[5120,128]{1,0:T(8,128)(2,1)} %refs_6_.1, bf16[5120,640]{1,0:T(8,128)(2,1)} %refs_7_.1), custom_call_target="tpu_custom_call" | custom-call | tf_op jit(solution)/shard_map/pallas_call | solution.py:309
  8.0 2.8 %collective-permute-start.4 = (bf16[512,896]{1,0:T(8,128)(2,1)}, bf16[512,896]{1,0:T(8,128)(2,1)}, u32[]{:S(2)}, u32[]{:S(2)}) collective-permute-start(bf16[512,896]{1,0:T(8,128)(2,1)} %get-tuple-element.27), channel_id=1, source_target_pairs={{48,0},{33,1},{50,2},{35,3},{52,4},{37,5},{54,6},{39,7},{56,8},{41... | collective-permute-start | bytes 2752520 | tf_op jit(solution)/shard_map/ppermute | solution.py:52
  11.4 10.0 %collective-permute-done.4.refs_8_ = bf16[512,896]{1,0:T(8,128)(2,1)} collective-permute-done((bf16[512,896]{1,0:T(8,128)(2,1)}, bf16[512,896]{1,0:T(8,128)(2,1)}, u32[]{:S(2)}, u32[]{:S(2)}) %collective-permute-start.4) | collective-permute-done | bytes 917536 | tf_op jit(solution)/shard_map/ppermute | solution.py:52
  21.4 5.6 %collective-permute-start.6 = (bf16[512,896]{1,0:T(8,128)(2,1)}, bf16[512,896]{1,0:T(8,128)(2,1)}, u32[]{:S(2)}, u32[]{:S(2)}) collective-permute-start(bf16[512,896]{1,0:T(8,128)(2,1)} %collective-permute-done.4.refs_8_), channel_id=1, source_target_pairs={{14,0},{3,1},{0,2},{5,3},{2,4},{7,5},{4,6},{9,7},{6,8},{11,9},{8,1... | collective-permute-start | bytes 2752520 | tf_op jit(solution)/shard_map/ppermute | solution.py:52
  27.0 4.3 %collective-permute-done.5.refs_9_ = bf16[512,896]{1,0:T(8,128)(2,1)} collective-permute-done((bf16[512,896]{1,0:T(8,128)(2,1)}, bf16[512,896]{1,0:T(8,128)(2,1)}, u32[]{:S(2)}, u32[]{:S(2)}) %collective-permute-start.5) | collective-permute-done | bytes 917536 | tf_op jit(solution)/shard_map/ppermute | solution.py:52
  31.3 5.6 %collective-permute-start.7 = (bf16[512,896]{1,0:T(8,128)(2,1)}, bf16[512,896]{1,0:T(8,128)(2,1)}, u32[]{:S(2)}, u32[]{:S(2)}) collective-permute-start(bf16[512,896]{1,0:T(8,128)(2,1)} %collective-permute-done.5.refs_9_), channel_id=1, source_target_pairs={{14,0},{3,1},{0,2},{5,3},{2,4},{7,5},{4,6},{9,7},{6,8},{11,9},{8,1... | collective-permute-start | bytes 2752520 | tf_op jit(solution)/shard_map/ppermute | solution.py:52
  36.9 2.8 %collective-permute-start.2 = (bf16[64,5120]{1,0:T(8,128)(2,1)S(1)}, bf16[64,5120]{1,0:T(8,128)(2,1)}, u32[]{:S(2)}, u32[]{:S(2)}) collective-permute-start(bf16[64,5120]{1,0:T(8,128)(2,1)S(1)} %slice.8), channel_id=1, source_target_pairs={{64,0},{65,1},{66,2},{67,3},{68,4},{69,5},{70,6},{71,7},{72,8},{73... | collective-permute-start | bytes 1966088 | tf_op jit(solution)/shard_map/ppermute | solution.py:52
  41.1 3.5 %collective-permute-start.9 = (bf16[512,896]{1,0:T(8,128)(2,1)}, bf16[512,896]{1,0:T(8,128)(2,1)}, u32[]{:S(2)}, u32[]{:S(2)}) collective-permute-start(bf16[512,896]{1,0:T(8,128)(2,1)} %collective-permute-done.4.refs_8_), channel_id=1, source_target_pairs={{1,0},{0,1},{3,2},{2,3},{5,4},{4,5},{7,6},{6,7},{9,8},{8,9},{11,10... | collective-permute-start | bytes 2752520 | tf_op jit(solution)/shard_map/ppermute | solution.py:52
  44.6 2.9 %collective-permute-done.7.refs_11_ = bf16[512,896]{1,0:T(8,128)(2,1)} collective-permute-done((bf16[512,896]{1,0:T(8,128)(2,1)}, bf16[512,896]{1,0:T(8,128)(2,1)}, u32[]{:S(2)}, u32[]{:S(2)}) %collective-permute-start.7) | collective-permute-done | bytes 917536 | tf_op jit(solution)/shard_map/ppermute | solution.py:52
  47.5 3.8 %collective-permute-start.13 = (bf16[512,896]{1,0:T(8,128)(2,1)}, bf16[512,896]{1,0:T(8,128)(2,1)}, u32[]{:S(2)}, u32[]{:S(2)}) collective-permute-start(bf16[512,896]{1,0:T(8,128)(2,1)} %collective-permute-done.8.refs_12_), channel_id=1, source_target_pairs={{1,0},{0,1},{3,2},{2,3},{5,4},{4,5},{7,6},{6,7},{9,8},{8,9},{11,10... | collective-permute-start | bytes 2752520 | tf_op jit(solution)/shard_map/ppermute | solution.py:52
  51.3 2.5 %collective-permute-done.2.top.refs_3_ = bf16[64,5120]{1,0:T(8,128)(2,1)} collective-permute-done((bf16[64,5120]{1,0:T(8,128)(2,1)S(1)}, bf16[64,5120]{1,0:T(8,128)(2,1)}, u32[]{:S(2)}, u32[]{:S(2)}) %collective-permute-start.2) | collective-permute-done | bytes 655392 | tf_op jit(solution)/shard_map/ppermute | solution.py:52
  53.8 3.7 %collective-permute-done.3.low.refs_4_ = bf16[64,5120]{1,0:T(8,128)(2,1)} collective-permute-done((bf16[64,5120]{1,0:T(8,128)(2,1)S(1)}, bf16[64,5120]{1,0:T(8,128)(2,1)}, u32[]{:S(2)}, u32[]{:S(2)}) %collective-permute-start.3) | collective-permute-done | bytes 655392 | tf_op jit(solution)/shard_map/ppermute | solution.py:52
  61.2 16.1 %shard_map.66 = (bf16[512,640]{1,0:T(8,128)(2,1)}, bf16[512,640]{1,0:T(8,128)(2,1)}, f32[512,256]{1,0:T(8,128)}, f32[512,256]{1,0:T(8,128)}, f32[16,640]{1,0:T(8,128)}) custom-call(s32[10]{0:T(128)} %pad_add_fusion.1.offsets, bf16[128,5120]{1,0:T(8,128)(2,1)} %bitcast.15, bf16[128,5120]{1,0:T(8,128)(2,1)} %copy-done.4, bf16[128,5120]{1,0:T(8,128)(2,1)} %copy-done.5, ...), custom_call_target="tpu_custom_call" | custom-call | flops 9395240960 | bytes 23592960 | tf_op jit(solution)/shard_map/pallas_call | solution.py:182
  78.9 2.5 %collective-permute-start.15 = (f32[16,640]{1,0:T(8,128)}, f32[16,640]{1,0:T(8,128)S(1)}, u32[]{:S(2)}, u32[]{:S(2)}) collective-permute-start(f32[16,640]{1,0:T(8,128)} %get-tuple-element.34), channel_id=1, source_target_pairs={{32,1},{33,2},{34,3},{35,4},{36,5},{37,6},{38,7},{39,8},{40,9},{41... | collective-permute-start | bytes 122888 | tf_op jit(solution)/shard_map/ppermute | solution.py:80
  81.4 3.0 %collective-permute-done.15.refs_5_ = f32[16,640]{1,0:T(8,128)S(1)} collective-permute-done((f32[16,640]{1,0:T(8,128)}, f32[16,640]{1,0:T(8,128)S(1)}, u32[]{:S(2)}, u32[]{:S(2)}) %collective-permute-start.15) | collective-permute-done | bytes 40992 | tf_op jit(solution)/shard_map/ppermute | solution.py:80
  88.6 3.0 %shard_map.67 = (bf16[512,640]{1,0:T(8,128)(2,1)S(1)}, bf16[512,640]{1,0:T(8,128)(2,1)S(1)}, f32[128,512]{1,0:T(8,128)S(1)}, f32[128,512]{1,0:T(8,128)S(1)}, f32...) custom-call(s32[3]{0:T(128)S(1)} %pad_add_fusion.place, bf16[512,640]{1,0:T(8,128)(2,1)S(1)} %copy-done, ...), custom_call_target="tpu_custom_call" | custom-call | flops 6000000000 | bytes 8000000 | tf_op jit(solution)/shard_map/pallas_call | solution.py:273
  93.3 2.0 %collective-permute-start.20 = (bf16[48,640]{1,0:T(8,128)(2,1)S(1)}, bf16[48,640]{1,0:T(8,128)(2,1)S(1)}, u32[]{:S(2)}, u32[]{:S(2)}) collective-permute-start(bf16[48,640]{1,0:T(8,128)(2,1)S(1)} %get-tuple-element.44), channel_id=1, source_target_pairs={{32,0},{33,1},{34,2},{35,3},{36,4},{37,5},{38,6},{39,7},{40,8},{41... | collective-permute-start | bytes 184328 | tf_op jit(solution)/shard_map/ppermute | solution.py:52
  95.2 2.2 %collective-permute-start.19 = (bf16[48,640]{1,0:T(8,128)(2,1)S(1)}, bf16[48,640]{1,0:T(8,128)(2,1)S(1)}, u32[]{:S(2)}, u32[]{:S(2)}) collective-permute-start(bf16[48,640]{1,0:T(8,128)(2,1)S(1)} %get-tuple-element.43), channel_id=1, source_target_pairs={{16,0},{17,1},{18,2},{19,3},{20,4},{21,5},{22,6},{23,7},{24,8},{25... | collective-permute-start | bytes 184328 | tf_op jit(solution)/shard_map/ppermute | solution.py:52
  98.2 1.6 %collective-permute-done.19 = bf16[48,640]{1,0:T(8,128)(2,1)S(1)} collective-permute-done((bf16[48,640]{1,0:T(8,128)(2,1)S(1)}, bf16[48,640]{1,0:T(8,128)(2,1)S(1)}, u32[]{:S(2)}, u32[]{:S(2)}) %collective-permute-start.19) | collective-permute-done | bytes 61472 | tf_op jit(solution)/shard_map/ppermute | solution.py:52
  99.8 2.0 %collective-permute-done.18 = bf16[48,640]{1,0:T(8,128)(2,1)S(1)} collective-permute-done((bf16[48,640]{1,0:T(8,128)(2,1)S(1)}, bf16[48,640]{1,0:T(8,128)(2,1)S(1)}, u32[]{:S(2)}, u32[]{:S(2)}) %collective-permute-start.18) | collective-permute-done | bytes 61472 | tf_op jit(solution)/shard_map/ppermute | solution.py:52
  101.8 3.8 %collective-permute-start.23 = (bf16[48,640]{1,0:T(8,128)(2,1)S(1)}, bf16[48,640]{1,0:T(8,128)(2,1)S(1)}, u32[]{:S(2)}, u32[]{:S(2)}) collective-permute-start(bf16[48,640]{1,0:T(8,128)(2,1)S(1)} %fusion), channel_id=1, source_target_pairs={{4,0},{5,1},{6,2},{7,3},{8,4},{9,5},{10,6},{11,7},{12,8},{13,9},{1... | collective-permute-start | bytes 184328 | tf_op jit(solution)/shard_map/ppermute | solution.py:52
  106.2 2.1 %collective-permute-start.21 = (bf16[48,640]{1,0:T(8,128)(2,1)S(1)}, bf16[48,640]{1,0:T(8,128)(2,1)S(1)}, u32[]{:S(2)}, u32[]{:S(2)}) collective-permute-start(bf16[48,640]{1,0:T(8,128)(2,1)S(1)} %fusion), channel_id=1, source_target_pairs={{2,0},{3,1},{4,2},{5,3},{6,4},{7,5},{8,6},{9,7},{10,8},{11,9},{12,... | collective-permute-start | bytes 184328 | tf_op jit(solution)/shard_map/ppermute | solution.py:52
  110.1 2.4 %collective-permute-start.24 = (bf16[48,640]{1,0:T(8,128)(2,1)S(1)}, bf16[48,640]{1,0:T(8,128)(2,1)S(1)}, u32[]{:S(2)}, u32[]{:S(2)}) collective-permute-start(bf16[48,640]{1,0:T(8,128)(2,1)S(1)} %get-tuple-element.49), channel_id=1, source_target_pairs={{8,0},{9,1},{10,2},{11,3},{12,4},{13,5},{14,6},{15,7},{0,8},{1,9},... | collective-permute-start | bytes 184328 | tf_op jit(solution)/shard_map/ppermute | solution.py:52
  112.5 4.8 %collective-permute-done.24 = bf16[48,640]{1,0:T(8,128)(2,1)S(1)} collective-permute-done((bf16[48,640]{1,0:T(8,128)(2,1)S(1)}, bf16[48,640]{1,0:T(8,128)(2,1)S(1)}, u32[]{:S(2)}, u32[]{:S(2)}) %collective-permute-start.24) | collective-permute-done | bytes 61472 | tf_op jit(solution)/shard_map/ppermute | solution.py:52
  119.0 4.1 %collective-permute-start.28 = (bf16[48,640]{1,0:T(8,128)(2,1)S(1)}, bf16[48,640]{1,0:T(8,128)(2,1)S(1)}, u32[]{:S(2)}, u32[]{:S(2)}) collective-permute-start(bf16[48,640]{1,0:T(8,128)(2,1)S(1)} %add_convert_fusion.refs_6_), channel_id=1, source_target_pairs={{1,0},{0,1},{3,2},{2,3},{5,4},{4,5},{7,6},{6,7},{9,8},{8,9},{11,10... | collective-permute-start | bytes 184328 | tf_op jit(solution)/shard_map/ppermute | solution.py:52
  123.1 1.8 %collective-permute-start.29 = (bf16[48,640]{1,0:T(8,128)(2,1)S(1)}, bf16[48,640]{1,0:T(8,128)(2,1)S(1)}, u32[]{:S(2)}, u32[]{:S(2)}) collective-permute-start(bf16[48,640]{1,0:T(8,128)(2,1)S(1)} %collective-permute-done.25.refs_7_), channel_id=1, source_target_pairs={{1,0},{0,1},{3,2},{2,3},{5,4},{4,5},{7,6},{6,7},{9,8},{8,9},{11,10... | collective-permute-start | bytes 184328 | tf_op jit(solution)/shard_map/ppermute | solution.py:52
  124.9 2.9 %collective-permute-start.30 = (bf16[48,640]{1,0:T(8,128)(2,1)S(1)}, bf16[48,640]{1,0:T(8,128)(2,1)S(1)}, u32[]{:S(2)}, u32[]{:S(2)}) collective-permute-start(bf16[48,640]{1,0:T(8,128)(2,1)S(1)} %collective-permute-done.26.refs_8_), channel_id=1, source_target_pairs={{1,0},{0,1},{3,2},{2,3},{5,4},{4,5},{7,6},{6,7},{9,8},{8,9},{11,10... | collective-permute-start | bytes 184328 | tf_op jit(solution)/shard_map/ppermute | solution.py:52
  129.1 3.0 %shard_map.69 = (bf16[128,1280]{1,0:T(8,128)(2,1)S(1)}, bf16[128,1280]{1,0:T(8,128)(2,1)S(1)}, bf16[128,1280]{1,0:T(8,128)(2,1)S(1)}, bf16[128,1280]{1,0:T(8,128)(2,1)S(1)}) custom-call(s32[1]{0:T(128)} %bitcast.1.place.y_place, s32[1]{0:T(128)} %bitcast.2.same, f32[128,512]{1,0:T(8,128)S(1)} %get-tuple-element.35.refs_0_, ...), custom_call_target="tpu_custom_call" | custom-call | tf_op jit(solution)/shard_map/pallas_call | solution.py:395
  133.6 7.5 %collective-permute-done.32.refs_1_ = bf16[128,1280]{1,0:T(8,128)(2,1)S(1)} collective-permute-done((bf16[128,1280]{1,0:T(8,128)(2,1)S(1)}, bf16[128,1280]{1,0:T(8,128)(2,1)S(1)}, u32[]{:S(2)}, u32[]{:S(2)}) %collective-permute-start.32) | collective-permute-done | bytes 327712 | tf_op jit(solution)/shard_map/ppermute | solution.py:52
  141.1 1.8 %collective-permute-done.33.refs_2_ = bf16[128,1280]{1,0:T(8,128)(2,1)S(1)} collective-permute-done((bf16[128,1280]{1,0:T(8,128)(2,1)S(1)}, bf16[128,1280]{1,0:T(8,128)(2,1)S(1)}, u32[]{:S(2)}, u32[]{:S(2)}) %collective-permute-start.33) | collective-permute-done | bytes 327712 | tf_op jit(solution)/shard_map/ppermute | solution.py:52
  142.9 8.0 %collective-permute-done.34.refs_3_ = bf16[128,1280]{1,0:T(8,128)(2,1)S(1)} collective-permute-done((bf16[128,1280]{1,0:T(8,128)(2,1)S(1)}, bf16[128,1280]{1,0:T(8,128)(2,1)S(1)}, u32[]{:S(2)}, u32[]{:S(2)}) %collective-permute-start.34) | collective-permute-done | bytes 327712 | tf_op jit(solution)/shard_map/ppermute | solution.py:52
  (75 shorter events, 22.8 us)
Async XLA Ops:
  0.0 36.8 %collective-permute-start = (bf16[128,5120]{1,0:T(8,128)(2,1)}, bf16[128,5120]{1,0:T(8,128)(2,1)S(1)}, u32[]{:S(2)}, u32[]{:S(2)}) collective-permute-start(bf16[128,5120]{1,0:T(8,128)(2,1)} %bitcast.13), channel_id=1, source_target_pairs={{64,0},{65,1},{66,2},{67,3},{68,4},{69,5},{70,6},{71,7},{72,8},{73... | collective-permute-start | bytes 3932168 | tf_op jit(solution)/shard_map/ppermute | solution.py:52
  3.3 36.3 %collective-permute-start.1 = (bf16[128,5120]{1,0:T(8,128)(2,1)}, bf16[128,5120]{1,0:T(8,128)(2,1)S(1)}, u32[]{:S(2)}, u32[]{:S(2)}) collective-permute-start(bf16[128,5120]{1,0:T(8,128)(2,1)} %bitcast.14), channel_id=1, source_target_pairs={{192,0},{193,1},{194,2},{195,3},{196,4},{197,5},{198,6},{199,7},{2... | collective-permute-start | bytes 3932168 | tf_op jit(solution)/shard_map/ppermute | solution.py:52
  8.0 13.5 %collective-permute-start.4 = (bf16[512,896]{1,0:T(8,128)(2,1)}, bf16[512,896]{1,0:T(8,128)(2,1)}, u32[]{:S(2)}, u32[]{:S(2)}) collective-permute-start(bf16[512,896]{1,0:T(8,128)(2,1)} %get-tuple-element.27), channel_id=1, source_target_pairs={{48,0},{33,1},{50,2},{35,3},{52,4},{37,5},{54,6},{39,7},{56,8},{41... | collective-permute-start | bytes 2752520 | tf_op jit(solution)/shard_map/ppermute | solution.py:52
  10.8 20.5 %collective-permute-start.5 = (bf16[512,896]{1,0:T(8,128)(2,1)}, bf16[512,896]{1,0:T(8,128)(2,1)}, u32[]{:S(2)}, u32[]{:S(2)}) collective-permute-start(bf16[512,896]{1,0:T(8,128)(2,1)} %get-tuple-element.28), channel_id=1, source_target_pairs={{48,0},{33,1},{50,2},{35,3},{52,4},{37,5},{54,6},{39,7},{56,8},{41... | collective-permute-start | bytes 2752520 | tf_op jit(solution)/shard_map/ppermute | solution.py:52
  11.2 29.8 %collective-permute-start.8 = (bf16[512,896]{1,0:T(8,128)(2,1)}, bf16[512,896]{1,0:T(8,128)(2,1)}, u32[]{:S(2)}, u32[]{:S(2)}) collective-permute-start(bf16[512,896]{1,0:T(8,128)(2,1)} %get-tuple-element.29), channel_id=1, source_target_pairs={{48,0},{33,1},{50,2},{35,3},{52,4},{37,5},{54,6},{39,7},{56,8},{41... | collective-permute-start | bytes 2752520 | tf_op jit(solution)/shard_map/ppermute | solution.py:52
  21.4 23.2 %collective-permute-start.6 = (bf16[512,896]{1,0:T(8,128)(2,1)}, bf16[512,896]{1,0:T(8,128)(2,1)}, u32[]{:S(2)}, u32[]{:S(2)}) collective-permute-start(bf16[512,896]{1,0:T(8,128)(2,1)} %collective-permute-done.4.refs_8_), channel_id=1, source_target_pairs={{14,0},{3,1},{0,2},{5,3},{2,4},{7,5},{4,6},{9,7},{6,8},{11,9},{8,1... | collective-permute-start | bytes 2752520 | tf_op jit(solution)/shard_map/ppermute | solution.py:52
  31.3 16.2 %collective-permute-start.7 = (bf16[512,896]{1,0:T(8,128)(2,1)}, bf16[512,896]{1,0:T(8,128)(2,1)}, u32[]{:S(2)}, u32[]{:S(2)}) collective-permute-start(bf16[512,896]{1,0:T(8,128)(2,1)} %collective-permute-done.5.refs_9_), channel_id=1, source_target_pairs={{14,0},{3,1},{0,2},{5,3},{2,4},{7,5},{4,6},{9,7},{6,8},{11,9},{8,1... | collective-permute-start | bytes 2752520 | tf_op jit(solution)/shard_map/ppermute | solution.py:52
  36.9 16.9 %collective-permute-start.2 = (bf16[64,5120]{1,0:T(8,128)(2,1)S(1)}, bf16[64,5120]{1,0:T(8,128)(2,1)}, u32[]{:S(2)}, u32[]{:S(2)}) collective-permute-start(bf16[64,5120]{1,0:T(8,128)(2,1)S(1)} %slice.8), channel_id=1, source_target_pairs={{64,0},{65,1},{66,2},{67,3},{68,4},{69,5},{70,6},{71,7},{72,8},{73... | collective-permute-start | bytes 1966088 | tf_op jit(solution)/shard_map/ppermute | solution.py:52
  39.7 17.8 %collective-permute-start.3 = (bf16[64,5120]{1,0:T(8,128)(2,1)S(1)}, bf16[64,5120]{1,0:T(8,128)(2,1)}, u32[]{:S(2)}, u32[]{:S(2)}) collective-permute-start(bf16[64,5120]{1,0:T(8,128)(2,1)S(1)} %slice.9), channel_id=1, source_target_pairs={{192,0},{193,1},{194,2},{195,3},{196,4},{197,5},{198,6},{199,7},{2... | collective-permute-start | bytes 1966088 | tf_op jit(solution)/shard_map/ppermute | solution.py:52
  41.1 18.8 %collective-permute-start.9 = (bf16[512,896]{1,0:T(8,128)(2,1)}, bf16[512,896]{1,0:T(8,128)(2,1)}, u32[]{:S(2)}, u32[]{:S(2)}) collective-permute-start(bf16[512,896]{1,0:T(8,128)(2,1)} %collective-permute-done.4.refs_8_), channel_id=1, source_target_pairs={{1,0},{0,1},{3,2},{2,3},{5,4},{4,5},{7,6},{6,7},{9,8},{8,9},{11,10... | collective-permute-start | bytes 2752520 | tf_op jit(solution)/shard_map/ppermute | solution.py:52
  44.6 15.6 %collective-permute-start.10 = (bf16[512,896]{1,0:T(8,128)(2,1)}, bf16[512,896]{1,0:T(8,128)(2,1)}, u32[]{:S(2)}, u32[]{:S(2)}) collective-permute-start(bf16[512,896]{1,0:T(8,128)(2,1)} %collective-permute-done.5.refs_9_), channel_id=1, source_target_pairs={{1,0},{0,1},{3,2},{2,3},{5,4},{4,5},{7,6},{6,7},{9,8},{8,9},{11,10... | collective-permute-start | bytes 2752520 | tf_op jit(solution)/shard_map/ppermute | solution.py:52
  47.5 12.7 %collective-permute-start.13 = (bf16[512,896]{1,0:T(8,128)(2,1)}, bf16[512,896]{1,0:T(8,128)(2,1)}, u32[]{:S(2)}, u32[]{:S(2)}) collective-permute-start(bf16[512,896]{1,0:T(8,128)(2,1)} %collective-permute-done.8.refs_12_), channel_id=1, source_target_pairs={{1,0},{0,1},{3,2},{2,3},{5,4},{4,5},{7,6},{6,7},{9,8},{8,9},{11,10... | collective-permute-start | bytes 2752520 | tf_op jit(solution)/shard_map/ppermute | solution.py:52
  53.8 6.5 %collective-permute-start.11 = (bf16[512,896]{1,0:T(8,128)(2,1)}, bf16[512,896]{1,0:T(8,128)(2,1)}, u32[]{:S(2)}, u32[]{:S(2)}) collective-permute-start(bf16[512,896]{1,0:T(8,128)(2,1)} %collective-permute-done.6.refs_10_), channel_id=1, source_target_pairs={{1,0},{0,1},{3,2},{2,3},{5,4},{4,5},{7,6},{6,7},{9,8},{8,9},{11,10... | collective-permute-start | bytes 2752520 | tf_op jit(solution)/shard_map/ppermute | solution.py:52
  59.9 21.5 %collective-permute-start.16 = (f32[4,640]{1,0:T(4,128)S(1)}, f32[4,640]{1,0:T(4,128)S(1)}, u32[]{:S(2)}, u32[]{:S(2)}) collective-permute-start(f32[4,640]{1,0:T(4,128)S(1)} %pad_maximum_fusion.refs_6_.refs_2_), channel_id=1, source_target_pairs={{32,0},{33,1},{34,2},{35,3},{36,4},{37,5},{38,6},{39,7},{40,8},{41... | collective-permute-start | bytes 30728 | tf_op jit(solution)/shard_map/ppermute | solution.py:52
  77.3 4.1 %collective-permute-start.14 = (f32[16,640]{1,0:T(8,128)}, f32[16,640]{1,0:T(8,128)S(1)}, u32[]{:S(2)}, u32[]{:S(2)}) collective-permute-start(f32[16,640]{1,0:T(8,128)} %get-tuple-element.34), channel_id=1, source_target_pairs={{32,0},{33,1},{34,2},{35,3},{36,4},{37,5},{38,6},{39,7},{40,8},{41... | collective-permute-start | bytes 122888 | tf_op jit(solution)/shard_map/ppermute | solution.py:52
  78.9 5.5 %collective-permute-start.15 = (f32[16,640]{1,0:T(8,128)}, f32[16,640]{1,0:T(8,128)S(1)}, u32[]{:S(2)}, u32[]{:S(2)}) collective-permute-start(f32[16,640]{1,0:T(8,128)} %get-tuple-element.34), channel_id=1, source_target_pairs={{32,1},{33,2},{34,3},{35,4},{36,5},{37,6},{38,7},{39,8},{40,9},{41... | collective-permute-start | bytes 122888 | tf_op jit(solution)/shard_map/ppermute | solution.py:80
  93.3 4.9 %collective-permute-start.20 = (bf16[48,640]{1,0:T(8,128)(2,1)S(1)}, bf16[48,640]{1,0:T(8,128)(2,1)S(1)}, u32[]{:S(2)}, u32[]{:S(2)}) collective-permute-start(bf16[48,640]{1,0:T(8,128)(2,1)S(1)} %get-tuple-element.44), channel_id=1, source_target_pairs={{32,0},{33,1},{34,2},{35,3},{36,4},{37,5},{38,6},{39,7},{40,8},{41... | collective-permute-start | bytes 184328 | tf_op jit(solution)/shard_map/ppermute | solution.py:52
  95.2 4.6 %collective-permute-start.19 = (bf16[48,640]{1,0:T(8,128)(2,1)S(1)}, bf16[48,640]{1,0:T(8,128)(2,1)S(1)}, u32[]{:S(2)}, u32[]{:S(2)}) collective-permute-start(bf16[48,640]{1,0:T(8,128)(2,1)S(1)} %get-tuple-element.43), channel_id=1, source_target_pairs={{16,0},{17,1},{18,2},{19,3},{20,4},{21,5},{22,6},{23,7},{24,8},{25... | collective-permute-start | bytes 184328 | tf_op jit(solution)/shard_map/ppermute | solution.py:52
  97.4 4.4 %collective-permute-start.18 = (bf16[48,640]{1,0:T(8,128)(2,1)S(1)}, bf16[48,640]{1,0:T(8,128)(2,1)S(1)}, u32[]{:S(2)}, u32[]{:S(2)}) collective-permute-start(bf16[48,640]{1,0:T(8,128)(2,1)S(1)} %get-tuple-element.42), channel_id=1, source_target_pairs={{48,0},{49,1},{50,2},{51,3},{52,4},{53,5},{54,6},{55,7},{56,8},{57... | collective-permute-start | bytes 184328 | tf_op jit(solution)/shard_map/ppermute | solution.py:52
  101.8 6.4 %collective-permute-start.23 = (bf16[48,640]{1,0:T(8,128)(2,1)S(1)}, bf16[48,640]{1,0:T(8,128)(2,1)S(1)}, u32[]{:S(2)}, u32[]{:S(2)}) collective-permute-start(bf16[48,640]{1,0:T(8,128)(2,1)S(1)} %fusion), channel_id=1, source_target_pairs={{4,0},{5,1},{6,2},{7,3},{8,4},{9,5},{10,6},{11,7},{12,8},{13,9},{1... | collective-permute-start | bytes 184328 | tf_op jit(solution)/shard_map/ppermute | solution.py:52
  105.6 4.3 %collective-permute-start.22 = (bf16[48,640]{1,0:T(8,128)(2,1)S(1)}, bf16[48,640]{1,0:T(8,128)(2,1)S(1)}, u32[]{:S(2)}, u32[]{:S(2)}) collective-permute-start(bf16[48,640]{1,0:T(8,128)(2,1)S(1)} %fusion), channel_id=1, source_target_pairs={{14,0},{15,1},{0,2},{1,3},{2,4},{3,5},{4,6},{5,7},{6,8},{7,9},{8,1... | collective-permute-start | bytes 184328 | tf_op jit(solution)/shard_map/ppermute | solution.py:52
  106.2 3.9 %collective-permute-start.21 = (bf16[48,640]{1,0:T(8,128)(2,1)S(1)}, bf16[48,640]{1,0:T(8,128)(2,1)S(1)}, u32[]{:S(2)}, u32[]{:S(2)}) collective-permute-start(bf16[48,640]{1,0:T(8,128)(2,1)S(1)} %fusion), channel_id=1, source_target_pairs={{2,0},{3,1},{4,2},{5,3},{6,4},{7,5},{8,6},{9,7},{10,8},{11,9},{12,... | collective-permute-start | bytes 184328 | tf_op jit(solution)/shard_map/ppermute | solution.py:52
  110.1 7.1 %collective-permute-start.24 = (bf16[48,640]{1,0:T(8,128)(2,1)S(1)}, bf16[48,640]{1,0:T(8,128)(2,1)S(1)}, u32[]{:S(2)}, u32[]{:S(2)}) collective-permute-start(bf16[48,640]{1,0:T(8,128)(2,1)S(1)} %get-tuple-element.49), channel_id=1, source_target_pairs={{8,0},{9,1},{10,2},{11,3},{12,4},{13,5},{14,6},{15,7},{0,8},{1,9},... | collective-permute-start | bytes 184328 | tf_op jit(solution)/shard_map/ppermute | solution.py:52
  117.2 5.8 %collective-permute-start.25 = (bf16[48,640]{1,0:T(8,128)(2,1)S(1)}, bf16[48,640]{1,0:T(8,128)(2,1)S(1)}, u32[]{:S(2)}, u32[]{:S(2)}) collective-permute-start(bf16[48,640]{1,0:T(8,128)(2,1)S(1)} %add_convert_fusion.refs_6_), channel_id=1, source_target_pairs={{32,0},{33,1},{34,2},{35,3},{36,4},{37,5},{38,6},{39,7},{40,8},{41... | collective-permute-start | bytes 184328 | tf_op jit(solution)/shard_map/ppermute | solution.py:52
  117.3 7.5 %collective-permute-start.26 = (bf16[48,640]{1,0:T(8,128)(2,1)S(1)}, bf16[48,640]{1,0:T(8,128)(2,1)S(1)}, u32[]{:S(2)}, u32[]{:S(2)}) collective-permute-start(bf16[48,640]{1,0:T(8,128)(2,1)S(1)} %add_convert_fusion.refs_6_), channel_id=1, source_target_pairs={{16,0},{17,1},{18,2},{19,3},{20,4},{21,5},{22,6},{23,7},{24,8},{25... | collective-permute-start | bytes 184328 | tf_op jit(solution)/shard_map/ppermute | solution.py:52
  118.3 9.5 %collective-permute-start.27 = (bf16[48,640]{1,0:T(8,128)(2,1)S(1)}, bf16[48,640]{1,0:T(8,128)(2,1)S(1)}, u32[]{:S(2)}, u32[]{:S(2)}) collective-permute-start(bf16[48,640]{1,0:T(8,128)(2,1)S(1)} %add_convert_fusion.refs_6_), channel_id=1, source_target_pairs={{48,0},{49,1},{50,2},{51,3},{52,4},{53,5},{54,6},{55,7},{56,8},{57... | collective-permute-start | bytes 184328 | tf_op jit(solution)/shard_map/ppermute | solution.py:52
  119.0 9.2 %collective-permute-start.28 = (bf16[48,640]{1,0:T(8,128)(2,1)S(1)}, bf16[48,640]{1,0:T(8,128)(2,1)S(1)}, u32[]{:S(2)}, u32[]{:S(2)}) collective-permute-start(bf16[48,640]{1,0:T(8,128)(2,1)S(1)} %add_convert_fusion.refs_6_), channel_id=1, source_target_pairs={{1,0},{0,1},{3,2},{2,3},{5,4},{4,5},{7,6},{6,7},{9,8},{8,9},{11,10... | collective-permute-start | bytes 184328 | tf_op jit(solution)/shard_map/ppermute | solution.py:52
  123.1 5.1 %collective-permute-start.29 = (bf16[48,640]{1,0:T(8,128)(2,1)S(1)}, bf16[48,640]{1,0:T(8,128)(2,1)S(1)}, u32[]{:S(2)}, u32[]{:S(2)}) collective-permute-start(bf16[48,640]{1,0:T(8,128)(2,1)S(1)} %collective-permute-done.25.refs_7_), channel_id=1, source_target_pairs={{1,0},{0,1},{3,2},{2,3},{5,4},{4,5},{7,6},{6,7},{9,8},{8,9},{11,10... | collective-permute-start | bytes 184328 | tf_op jit(solution)/shard_map/ppermute | solution.py:52
  124.9 3.8 %collective-permute-start.30 = (bf16[48,640]{1,0:T(8,128)(2,1)S(1)}, bf16[48,640]{1,0:T(8,128)(2,1)S(1)}, u32[]{:S(2)}, u32[]{:S(2)}) collective-permute-start(bf16[48,640]{1,0:T(8,128)(2,1)S(1)} %collective-permute-done.26.refs_8_), channel_id=1, source_target_pairs={{1,0},{0,1},{3,2},{2,3},{5,4},{4,5},{7,6},{6,7},{9,8},{8,9},{11,10... | collective-permute-start | bytes 184328 | tf_op jit(solution)/shard_map/ppermute | solution.py:52
  132.1 9.0 %collective-permute-start.32 = (bf16[128,1280]{1,0:T(8,128)(2,1)S(1)}, bf16[128,1280]{1,0:T(8,128)(2,1)S(1)}, u32[]{:S(2)}, u32[]{:S(2)}) collective-permute-start(bf16[128,1280]{1,0:T(8,128)(2,1)S(1)} %get-tuple-element.46), channel_id=1, source_target_pairs={{64,0},{65,1},{66,2},{67,3},{68,4},{69,5},{70,6},{71,7},{72,8},{73... | collective-permute-start | bytes 983048 | tf_op jit(solution)/shard_map/ppermute | solution.py:52
  132.7 10.2 %collective-permute-start.33 = (bf16[128,1280]{1,0:T(8,128)(2,1)S(1)}, bf16[128,1280]{1,0:T(8,128)(2,1)S(1)}, u32[]{:S(2)}, u32[]{:S(2)}) collective-permute-start(bf16[128,1280]{1,0:T(8,128)(2,1)S(1)} %get-tuple-element.47), channel_id=1, source_target_pairs={{128,0},{129,1},{130,2},{131,3},{132,4},{133,5},{134,6},{135,7},{1... | collective-permute-start | bytes 983048 | tf_op jit(solution)/shard_map/ppermute | solution.py:52
  132.7 18.2 %collective-permute-start.34 = (bf16[128,1280]{1,0:T(8,128)(2,1)S(1)}, bf16[128,1280]{1,0:T(8,128)(2,1)S(1)}, u32[]{:S(2)}, u32[]{:S(2)}) collective-permute-start(bf16[128,1280]{1,0:T(8,128)(2,1)S(1)} %get-tuple-element.48), channel_id=1, source_target_pairs={{192,0},{193,1},{194,2},{195,3},{196,4},{197,5},{198,6},{199,7},{2... | collective-permute-start | bytes 983048 | tf_op jit(solution)/shard_map/ppermute | solution.py:52
  (12 other events, 108.0 us)
